TPU v7x, 256 devices: a whole 4x4x8 slice. The times are simulated.
256 devices in a mesh: row: 32 (over y, z), col: 4 (over x), rep: 2 (over core).
Axes of the slice: x: 4, y: 4, z: 8, core: 2. Of those that a mesh axis runs over, the one named last changes fastest.
Arguments:
- tiles: float32 [32, 4, 32, 128, 128], P('row', 'col'), may hold values from -6 to 6
- block_row: int32 [32, 4, 32], P('row', 'col'), may hold values from 0 to 23
- block_col: int32 [32, 4, 32], P('row', 'col'), may hold values from 0 to 39
- live_rows: int32 [32, 4, 32], P('row', 'col'), may hold values from 0 to 128
- omega: float32 [4, 5120, 256], P('col', 'row', 'rep'), may hold values from -6 to 6
Outputs:
- basis: float32 [32, 3072, 256], P('row', 'col', 'rep')
- panel_basis: float32 [4, 5120, 256], P('col', 'row', 'rep')
Inputs may be any that keep to these rules, and one draw needn't show every extreme that they name: A slot with live_rows 0 holds nothing; slots may repeat a block, and then add.
All inputs are finite; a program needn't handle non-finite values.
Results may differ from a plain program's by a relative error of at most 0.0003.
Values sent between devices are 32-bit elements; how exact they have to be, the bound alone decides.
No kernel may reach another device: no remote copies, remote signals or barrier semaphores. Data moves between devices by JAX's collectives and lax.ppermute only.
A program may use at most 128 MiB of HBM per device.

v0:
```python
import math

import jax
import jax.numpy as jnp
from jax import lax
from jax.experimental import pallas as pl
from jax.experimental.pallas import tpu as pltpu
from jax.sharding import Mesh
from jax.sharding import PartitionSpec as P

ITERS = 2
RB_DEV = 24
CB_DEV = 40
BS = 128
HALF = 128
NY = 4
NZ = 8
NX = 4
ROWS_OWN = 768
COLS_OWN = 160
UNROLL = 8
F32 = jnp.float32
BF16 = jnp.bfloat16
VMEM_LIMIT = 16 * 1024 * 1024


def dot_nn(a, b):
    return lax.dot_general(
        a, b, (((1,), (0,)), ((), ())), precision=lax.Precision.HIGHEST, preferred_element_type=F32
    )


def dot_nt(a, b):
    return lax.dot_general(
        a, b, (((1,), (1,)), ((), ())), precision=lax.Precision.HIGHEST, preferred_element_type=F32
    )


def dot_tn(a, b):
    return lax.dot_general(
        a, b, (((0,), (0,)), ((), ())), precision=lax.Precision.HIGHEST, preferred_element_type=F32
    )


def split(x):
    high = x.astype(BF16)
    return high, (x - high.astype(F32)).astype(BF16)


def product_of(a, b, dims):
    (axis_a,), (axis_b,) = dims
    pair = jnp.concatenate(split(b), axis=1 - axis_b)
    both = lax.dot_general(
        jnp.concatenate(split(a), axis=axis_a),
        jnp.concatenate([pair, pair], axis=axis_b),
        (dims, ((), ())),
        preferred_element_type=F32,
    )
    return both[:, :HALF] + both[:, HALF:]


def masked_tile(tiles, slots, slot):
    iota = lax.broadcasted_iota(jnp.int32, (BS, BS), 0)
    return jnp.where(iota < slots[2, slot], tiles[slot], F32(0.0))


def block_at(index):
    return pl.ds(pl.multiple_of(index * BS, BS), BS)


def accumulate(slots, held, total, source, target, shift, count, tiles, dims):
    def body(step, carry):
        base = step * UNROLL
        products = []
        for offset in range(UNROLL):
            slot = base + offset
            tile = masked_tile(tiles, slots, slot)
            products.append(product_of(tile, held[block_at(slots[source, slot]), :], dims))
        for offset in range(UNROLL):
            place = lax.rem(slots[target, base + offset] + (count - shift), count)
            total[block_at(place), :] += products[offset]
        return carry

    total[...] = jnp.zeros_like(total)
    lax.fori_loop(0, tiles.shape[0] // UNROLL, body, 0)


def forward_kernel(
    pos, slots, tiles, line, before, after, far_a, far_b, carried, o0, o1, o2, o3, passed, held, total
):
    y, z, x = pos[0], pos[1], pos[2]
    passed[...] = carried[...]
    half = NZ // 2
    parts = [(0, line, 0), (NY - 1, before, 0), (1, after, 0), (2, far_a, 0), (2, far_b, half)]
    for shift, ref, first in parts:
        from_y = lax.rem(y + shift, NY)
        for k in range(ref.shape[0] // COLS_OWN):
            from_z = lax.rem(z + (half + first + k), NZ)
            place = pl.multiple_of((from_y * NZ + from_z) * COLS_OWN, 32)
            held[pl.ds(place, COLS_OWN), :] = ref[k * COLS_OWN : (k + 1) * COLS_OWN, :]
    accumulate(slots, held, total, 1, 0, x * (RB_DEV // NX), RB_DEV, tiles, ((1,), (0,)))
    for k, out in enumerate((o0, o1, o2, o3)):
        out[...] = total[k * ROWS_OWN : (k + 1) * ROWS_OWN, :]


def backward_kernel(
    pos, slots, tiles, p0, p1, p2, p3, carried, o0, o1, far_a, far_b, o3, held, total
):
    y, x = pos[0], pos[2]
    for j, piece in enumerate((p0, p1, p2, p3)):
        from_x = lax.rem(x + (NX - j), NX)
        held[pl.ds(pl.multiple_of(from_x * ROWS_OWN, 256), ROWS_OWN), :] = piece[...]
    accumulate(slots, held, total, 0, 1, y * (CB_DEV // NY), CB_DEV, tiles, ((0,), (0,)))
    big, half = o0.shape[0], o0.shape[0] // 2
    o0[...] = total[0:big, :]
    o1[...] = total[big : 2 * big, :]
    o3[...] = total[3 * big :, :]
    for out, start in ((far_a, 2 * big), (far_b, 2 * big + half)):
        out[0:half, :] = total[start : start + half, :]
        out[half:, :] = carried[...]


def pair_kernel(up, own, down, low, high):
    low[0:COLS_OWN, :] = up[...]
    low[COLS_OWN:, :] = own[...]
    high[0:COLS_OWN, :] = own[...]
    high[COLS_OWN:, :] = down[...]


def fan_kernel(up, own, down, parts, low, high, total):
    pair_kernel(up, own, down, low, high)
    value = parts[0]
    for k in range(1, parts.shape[0]):
        value = value + parts[k]
    total[...] = value


def join_kernel(*refs):
    *pieces, before, line = refs
    start = 0
    for piece in pieces:
        line[start : start + piece.shape[0], :] = piece[...]
        start += piece.shape[0]


def copies_kernel(a, b, c, d, copies):
    total = (a[...] + c[...]) + (b[...] + d[...])
    for k in range(copies.shape[0]):
        copies[k] = total


def cut_kernel(after_that, back, before, first, last):
    size = first.shape[0]
    first[...] = after_that[0:size, :]
    last[...] = back[size:, :]


def relay_y_kernel(near, far_a, back, far_b, own_part, far_part, to_near, to_back, copies):
    size = near.shape[0] // 2
    to_near[0:size, :] = near[0:size, :] + far_a[0:size, :]
    to_near[size:, :] = near[size:, :]
    to_back[0:size, :] = back[0:size, :]
    to_back[size:, :] = back[size:, :] + far_b[0:size, :]
    total = (own_part[...] + far_part[...]) + (far_a[size:, :] + far_b[size:, :])
    for k in range(copies.shape[0]):
        copies[k] = total


def split_z_kernel(pos, own, before, after, carried, up, down, mine, near, back, passed):
    passed[...] = carried[...]
    z = pos[1]

    def piece(shift):
        place = pl.ds(pl.multiple_of(lax.rem(z + shift, NZ) * COLS_OWN, 32), COLS_OWN)
        return own[place, :] + (before[place, :] + after[place, :])

    for k, shift in enumerate((2, 3, 4)):
        up[k * COLS_OWN : (k + 1) * COLS_OWN, :] = piece(shift)
    for k, shift in enumerate((5, 6)):
        down[k * COLS_OWN : (k + 1) * COLS_OWN, :] = piece(shift)
    mine[...] = piece(0)
    near[...] = piece(1)
    back[...] = piece(NZ - 1)


def relay_z_kernel(mine, near, back, up, down, before, to_mine, to_near, to_back):
    to_back[...] = back[...] + up[0:COLS_OWN, :]
    to_mine[...] = mine[...] + (up[COLS_OWN : 2 * COLS_OWN, :] + down[0:COLS_OWN, :])
    to_near[...] = near[...] + (up[2 * COLS_OWN :, :] + down[COLS_OWN:, :])


def sum_kernel(a, b, c, d, before, out):
    out[...] = (a[...] + c[...]) + (b[...] + d[...])


def sum_three_kernel(a, b, c, out):
    out[...] = a[...] + (b[...] + c[...])


def halves(pos, own, other):
    first = pos[3] == 0
    a, b = own[...], other[...]
    return jnp.where(first, a, b), jnp.where(first, b, a)


def gram_kernel(pos, own, other, gram):
    left, right = halves(pos, own, other)
    mine = own[...]
    gram[0:HALF, :] = dot_tn(left, mine)
    gram[HALF:, :] = dot_tn(right, mine)


def applied(pos, own, other, inv):
    left, right = halves(pos, own, other)
    dims = ((1,), (1,))
    new_left = product_of(left, inv[0:HALF, 0:HALF], dims)
    new_right = product_of(left, inv[HALF:, 0:HALF], dims) + product_of(
        right, inv[HALF:, HALF:], dims
    )
    return new_left, new_right


def apply_gram_kernel(pos, own, other, inv, out, out_other, gram):
    new_left, new_right = applied(pos, own, other, inv)
    first = pos[3] == 0
    mine = jnp.where(first, new_left, new_right)
    out[...] = mine
    out_other[...] = jnp.where(first, new_right, new_left)
    gram[0:HALF, :] = dot_tn(new_left, mine)
    gram[HALF:, :] = dot_tn(new_right, mine)


def make_apply_scaled(scale):
    def apply_scaled_kernel(pos, own, other, inv, out):
        new_left, new_right = applied(pos, own, other, inv)
        out[...] = jnp.where(pos[3] == 0, new_left, new_right) * F32(scale)

    return apply_scaled_kernel


WIDE = 16


def thirds(x):
    high = x.astype(BF16).astype(F32)
    rest = x - high
    middle = rest.astype(BF16).astype(F32)
    return high, middle, rest - middle


def inverse_factor(matrix):
    size = matrix.shape[0]
    lane = lax.broadcasted_iota(jnp.int32, (WIDE, size), 1)
    sub = lax.broadcasted_iota(jnp.int32, (WIDE, size), 0)
    all_lanes = lax.broadcasted_iota(jnp.int32, (size, size), 1)

    def spread(column):
        return jnp.broadcast_to(column, (WIDE, size))

    def body(step, array):
        rest = size - WIDE * step
        top = array[0:WIDE, :]
        cols = [spread(top[:, j : j + 1]) for j in range(WIDE)]
        upper = jnp.zeros((WIDE, size), F32)
        for j in range(WIDE):
            root = lax.rsqrt(spread(cols[j][j : j + 1, :]))
            line = jnp.where(lane == j, root, spread(top[j : j + 1, :]) * root)
            factor = jnp.where(sub > j, cols[j] * root, 0.0)
            for later in range(j + 1, WIDE):
                entry = spread(cols[later][j : j + 1, :]) * root
                cols[later] = cols[later] - factor * entry
            top = jnp.where((lane == j) & (sub > j), 0.0, top) - factor * line
            upper = jnp.where(sub == j, line, upper)
        done = jnp.where((lane > sub) & (lane < rest), 0.0, upper)
        a, b, c = thirds(jnp.where((lane >= WIDE) & (lane < rest), upper, 0.0))
        p, q, r = thirds(jnp.where((lane < WIDE) & (lane > sub), 0.0, upper))
        left = jnp.concatenate([a, a, b, a, b, c], axis=0).astype(BF16)
        right = jnp.concatenate([p, q, p, r, q, p], axis=0).astype(BF16)
        change = lax.dot_general(
            left, right, (((0,), (0,)), ((), ())), preferred_element_type=F32
        )
        array = jnp.where(all_lanes < WIDE, 0.0, array) - change
        return pltpu.roll(jnp.concatenate([array[WIDE:], done], axis=0), size - WIDE, 1)

    return lax.fori_loop(0, size // WIDE, body, matrix)


def factor_kernel(pos, own, other, inv):
    first = pos[3] == 0
    a, b = own[...], other[...]
    left = jnp.where(first, a, b)
    corner = jnp.where(first, b, a)[HALF:, :]
    inv_first = inverse_factor(left[0:HALF, :])
    below = left[HALF:, :]
    low = dot_nt(below, inv_first)
    inv_last = inverse_factor(corner - dot_nt(low, low))
    inv[0:HALF, 0:HALF] = inv_first
    inv[0:HALF, HALF:] = jnp.zeros((HALF, HALF), F32)
    inv[HALF:, 0:HALF] = -dot_nn(inv_last, dot_nn(low, inv_first))
    inv[HALF:, HALF:] = inv_last


def call(kernel, shapes, scalars, arrays, scratch=(), before=()):
    smem = pl.BlockSpec(memory_space=pltpu.SMEM)
    vmem = pl.BlockSpec(memory_space=pltpu.VMEM)
    anywhere = pl.BlockSpec(memory_space=pl.ANY)
    return pl.pallas_call(
        kernel,
        out_shape=[jax.ShapeDtypeStruct(shape, F32) for shape in shapes],
        in_specs=[smem] * len(scalars) + [vmem] * len(arrays) + [anywhere] * len(before),
        out_specs=[vmem] * len(shapes),
        scratch_shapes=[pltpu.VMEM(shape, F32) for shape in scratch],
        compiler_params=pltpu.CompilerParams(vmem_limit_bytes=VMEM_LIMIT),
        cost_estimate=pl.CostEstimate(flops=1000000, bytes_accessed=100000, transcendentals=0),
    )(*scalars, *arrays, *before)


def ring(size, shift):
    return [(i, (i + shift) % size) for i in range(size)]


def send(value, axis, shift):
    size = {"y": NY, "z": NZ, "col": NX, "rep": 2}[axis]
    return lax.ppermute(value, axis, ring(size, shift))


def shards(tiles, block_row, block_col, live_rows, omega):
    local_tiles = tiles[0, 0]
    slots = jnp.concatenate([block_row[0], block_col[0], live_rows[0]], axis=0)
    pos = jnp.stack([lax.axis_index(a) for a in ("y", "z", "col", "rep")]).astype(jnp.int32)
    big = CB_DEV // NY * BS
    grams = (2 * HALF, HALF)
    chunks = (NZ, 2 * HALF // NZ, HALF)

    def sum_ring(value, axis, before=pos):
        got = [value] + [send(value, axis, k) for k in range(1, 4)]
        return call(sum_kernel, [value.shape], [], got, (), [before])[0]

    def exchange_z(parts):
        return lax.all_to_all(parts, "z", 0, 0)

    def spread_y(line, done):
        before, after = send(line, "y", 1), send(line, "y", NY - 1)
        first, last = call(cut_kernel, [(big // 2, HALF)] * 2, [], [before, after], (), [done])
        return [line, before, after, send(first, "y", 1), send(last, "y", NY - 1)]

    def gather_first(own):
        up, down, far = (send(own, "z", k) for k in (1, NZ - 1, 4))
        low, high = call(pair_kernel, [(2 * COLS_OWN, HALF)] * 2, [], [up, own, down])
        line = [far, send(low, "z", 2), up, own, down, send(high, "z", NZ - 2)]
        return spread_y(call(join_kernel, [(big, HALF)], [], line, (), [pos])[0], pos)

    def gather_panel(own, gram):
        up, down, far = (send(own, "z", k) for k in (1, NZ - 1, 4))
        parts = exchange_z(gram.reshape(chunks))
        low, high, part = call(
            fan_kernel, [(2 * COLS_OWN, HALF)] * 2 + [chunks[1:]], [], [up, own, down, parts]
        )
        line = [far, send(low, "z", 2), up, own, down, send(high, "z", NZ - 2)]
        part = sum_ring(part, "y")
        parts = [part] + [send(part, "col", k) for k in range(1, NX)]
        line = call(join_kernel, [(big, HALF)], [], line, (), [part])[0]
        copies = call(copies_kernel, [chunks], [], parts)[0]
        whole = exchange_z(copies).reshape(grams)
        return spread_y(line, whole), whole

    def gather_rows(own):
        return [own] + [send(own, "col", k) for k in range(1, NX)]

    def forward(pieces, carried):
        *out, passed = call(
            forward_kernel,
            [(ROWS_OWN, HALF)] * NX + [carried.shape],
            [pos, slots],
            [local_tiles, *pieces, carried],
            [(CB_DEV * BS, HALF), (RB_DEV * BS, HALF)],
        )
        return [out[0]] + [send(out[k], "col", k) for k in range(1, NX)], passed

    def forward_sum(got, before):
        return call(sum_kernel, [(ROWS_OWN, HALF)], [], got, (), [before])[0]

    def backward(pieces, gram):
        part = sum_ring(jnp.sum(exchange_z(gram.reshape(chunks)), axis=0), "col")
        far = (big // 2 + part.shape[0], HALF)
        far_part = send(part, "y", 2)
        own, near, far_a, far_b, back = call(
            backward_kernel,
            [(big, HALF)] * 2 + [far] * 2 + [(big, HALF)],
            [pos, slots],
            [local_tiles, *pieces, part],
            [(RB_DEV * BS, HALF), (CB_DEV * BS, HALF)],
        )
        far_a, far_b = send(far_a, "y", 1), send(far_b, "y", NY - 1)
        near, back, copies = call(
            relay_y_kernel,
            [(big, HALF)] * 2 + [chunks],
            [],
            [near, far_a, back, far_b, part, far_part],
        )
        before, after = send(near, "y", 1), send(back, "y", NY - 1)
        mine = exchange_z(copies).reshape(grams)
        piece = (COLS_OWN, HALF)
        up, down, own, near, back, mine = call(
            split_z_kernel,
            [(3 * COLS_OWN, HALF), (2 * COLS_OWN, HALF), piece, piece, piece, grams],
            [pos],
            [own, before, after, mine],
        )
        up, down = send(up, "z", 3), send(down, "z", NZ - 3)
        inv = factor(mine, send(mine, "rep", 1))
        own, near, back = call(
            relay_z_kernel, [piece] * 3, [], [own, near, back, up, down], (), [inv]
        )
        got = [own, send(near, "z", 1), send(back, "z", NZ - 1)]
        return call(sum_three_kernel, [piece], [], got)[0], inv

    def sum_gram(gram):
        count, chunk = NY * NX, 2 * HALF // (NY * NX)
        parts = lax.all_to_all(gram.reshape(count, chunk, HALF), ("y", "col"), 0, 0)
        part = jnp.sum(parts, axis=0)
        parts = lax.all_to_all(jnp.broadcast_to(part[None], (NZ, chunk, HALF)), "z", 0, 0)
        part = jnp.sum(parts, axis=0)
        whole = lax.all_to_all(
            jnp.broadcast_to(part[None], (count, chunk, HALF)), ("y", "col"), 0, 0
        )
        return whole.reshape(grams)

    def factor(mine, other):
        return call(factor_kernel, [(2 * HALF, 2 * HALF)], [pos], [mine, other])[0]

    def normalised(value, inv):
        other = send(value, "rep", 1)
        shape = value.shape
        return call(apply_gram_kernel, [shape, shape, grams], [pos], [value, other, inv])

    def finished(value, other, inv, scale):
        return call(make_apply_scaled(scale), [value.shape], [pos], [value, other, inv])[0]

    got, _ = forward(gather_first(omega[0]), omega[0, 0:8])
    own = forward_sum(got, pos)
    gram = call(gram_kernel, [grams], [pos], [own, send(own, "rep", 1)])[0]
    total_rows = ROWS_OWN * NX * NY * NZ
    total_cols = COLS_OWN * NX * NY * NZ
    for step in range(ITERS):
        value, inv = backward(gather_rows(own), gram)
        panel, panel_other, gram = normalised(value, inv)
        pieces, mine = gather_panel(panel, gram)
        got, other = forward(pieces, send(mine, "rep", 1))
        inv = factor(mine, other)
        if step == ITERS - 1:
            panel_basis = finished(panel, panel_other, inv, math.sqrt(total_cols))
        own, other, gram = normalised(
            forward_sum(got, panel_basis if step == ITERS - 1 else inv), inv
        )
    mine = sum_gram(gram)
    inv = factor(mine, send(mine, "rep", 1))
    basis = finished(own, other, inv, math.sqrt(total_rows))
    return basis[None], panel_basis[None]


def solution(mesh):
    fine = Mesh(mesh.devices.reshape(NY, NZ, NX, 2), ("y", "z", "col", "rep"))
    row = ("y", "z")
    placed = (
        P(row, "col", None, None, None),
        P(row, "col", None),
        P(row, "col", None),
        P(row, "col", None),
        P("col", row, "rep"),
    )
    return jax.shard_map(
        shards,
        mesh=fine,
        in_specs=placed,
        out_specs=(P(row, "col", "rep"), P("col", row, "rep")),
        check_vma=False,
    )
```

profile of v0, /device:TPU:1, one launch (start us, length us, event | category | flops | bytes accessed | tf_op | source)
XLA Modules:
  0.0 469.0 jit_solution(11272237729396058023)
XLA Ops:
  0.7 6.5 %collective-permute-start.2 = (f32[160,128]{1,0:T(8,128)}, f32[160,128]{1,0:T(8,128)S(1)}, u32[]{:S(2)}, u32[]{:S(2)}) collective-permute-start(f32[160,128]{1,0:T(8,128)} %bitcast.8.own.refs_3_), channel_id=1, source_target_pairs={{0,56},{8,0},{16,8},{24,16},{32,24},{40,32},{48,40},{56,48},{1,57}... | collective-permute-start | bytes 245768 | tf_op jit(solution)/shard_map/ppermute | solution.py:324
  9.0 2.9 collective-permute-done.1.up.refs_2_
  12.9 3.6 collective-permute-start.4
  17.9 6.6 %collective-permute-done.refs_0_ = f32[160,128]{1,0:T(8,128)S(1)} collective-permute-done((f32[160,128]{1,0:T(8,128)}, f32[160,128]{1,0:T(8,128)S(1)}, u32[]{:S(2)}, u32[]{:S(2)}) %collective-permute-start) | collective-permute-done | bytes 81952 | tf_op jit(solution)/shard_map/ppermute | solution.py:324
  28.3 10.0 %collective-permute-done.6.back.after = f32[1280,128]{1,0:T(8,128)S(1)} collective-permute-done((f32[1280,128]{1,0:T(8,128)S(1)}, f32[1280,128]{1,0:T(8,128)S(1)}, u32[]{:S(2)}, u32[]{:S(2)}) %collective-permute-start.6) | collective-permute-done | bytes 655392 | tf_op jit(solution)/shard_map/ppermute | solution.py:324
  38.3 3.1 collective-permute-done.5.after_that.before
  45.0 4.5 collective-permute-done.7.far_a
  57.1 3.0 collective-permute-done.9.b
  60.1 6.8 %collective-permute-done.10.c = f32[768,128]{1,0:T(8,128)S(1)} collective-permute-done((f32[768,128]{1,0:T(8,128)S(1)}, f32[768,128]{1,0:T(8,128)S(1)}, u32[]{:S(2)}, u32[]{:S(2)}) %collective-permute-start.10) | collective-permute-done | bytes 393248 | tf_op jit(solution)/shard_map/ppermute | solution.py:324
  67.0 7.6 %collective-permute-start.15 = (f32[768,128]{1,0:T(8,128)S(1)}, f32[768,128]{1,0:T(8,128)S(1)}, u32[]{:S(2)}, u32[]{:S(2)}) collective-permute-start(f32[768,128]{1,0:T(8,128)S(1)} %shard_map.72.own.p0), channel_id=1, source_target_pairs={{0,1},{1,0},{2,3},{3,2},{4,5},{5,4},{6,7},{7,6},{8,9},{9,8},{10,11... | collective-permute-start | bytes 1179656 | tf_op jit(solution)/shard_map/ppermute | solution.py:324
  79.6 16.0 %all_to_all.55 = f32[8,32,128]{2,1,0:T(8,128)S(1)} all-to-all(f32[8,32,128]{2,1,0:T(8,128)S(1)} %bitcast.38), channel_id=1, replica_groups=mesh['y'=4,'z'=8,'col'=4,'rep'=2] {'z'}, dimensions={0} | all-to-all | bytes 262144 | tf_op jit(solution)/shard_map/all_to_all | solution.py:340
  109.5 4.8 %collective-permute-done.21.far_part = f32[32,128]{1,0:T(8,128)S(1)} collective-permute-done((f32[32,128]{1,0:T(8,128)S(1)}, f32[32,128]{1,0:T(8,128)S(1)}, u32[]{:S(2)}, u32[]{:S(2)}) %collective-permute-start.21) | collective-permute-done | bytes 16416 | tf_op jit(solution)/shard_map/ppermute | solution.py:324
  117.2 13.3 %all_to_all.56 = f32[8,32,128]{2,1,0:T(8,128)S(1)} all-to-all(f32[8,32,128]{2,1,0:T(8,128)S(1)} %get-tuple-element.89), channel_id=1, replica_groups=mesh['y'=4,'z'=8,'col'=4,'rep'=2] {'z'}, dimensions={0} | all-to-all | bytes 262144 | tf_op jit(solution)/shard_map/all_to_all | solution.py:340
  131.3 4.4 collective-permute-start.25
  135.7 5.7 %collective-permute-start.26 = (f32[256,128]{1,0:T(8,128)S(1)}, f32[256,128]{1,0:T(8,128)S(1)}, u32[]{:S(2)}, u32[]{:S(2)}) collective-permute-start(f32[256,128]{1,0:T(8,128)S(1)} %get-tuple-element.95.own), channel_id=1, source_target_pairs={{0,1},{1,0},{2,3},{3,2},{4,5},{5,4},{6,7},{7,6},{8,9},{9,8},{10,11... | collective-permute-start | bytes 393224 | tf_op jit(solution)/shard_map/ppermute | solution.py:324
  142.4 10.6 %shard_map.78.before.inv = f32[256,256]{1,0:T(8,128)S(1)} custom-call(s32[4]{0:T(128)S(1)} %pad_add_fusion.1.refs_6_.before.pos, f32[256,128]{1,0:T(8,128)S(1)} %get-tuple-element.95.own, f32[256,128]{1,0:T(8,128)S(1)} %collective-permute-done.26.other), custom_call_target="tpu_custom_call" | custom-call | flops 1000000 | bytes 100000 | tf_op jit(solution)/shard_map/pallas_call | solution.py:307
  162.1 4.3 all-to-all-start.2
  169.1 3.0 collective-permute-done.32.down.refs_4_
  174.5 3.6 collective-permute-start.34
  178.0 3.0 collective-permute-start.30
  184.1 3.2 collective-permute-done.36.c
  190.0 5.4 %collective-permute-start.42 = (f32[32,128]{1,0:T(8,128)S(1)}, f32[32,128]{1,0:T(8,128)S(1)}, u32[]{:S(2)}, u32[]{:S(2)}) collective-permute-start(f32[32,128]{1,0:T(8,128)S(1)} %shard_map.83.refs_6_.a), channel_id=1, source_target_pairs={{0,6},{2,0},{4,2},{6,4},{1,7},{3,1},{5,3},{7,5},{8,14},{10,8},{12,... | collective-permute-start | bytes 49160 | tf_op jit(solution)/shard_map/ppermute | solution.py:324
  196.3 3.2 collective-permute-done.41.c
  199.5 14.0 %all_to_all.57 = f32[8,32,128]{2,1,0:T(8,128)S(1)} all-to-all(f32[8,32,128]{2,1,0:T(8,128)S(1)} %shard_map.85), channel_id=1, replica_groups=mesh['y'=4,'z'=8,'col'=4,'rep'=2] {'z'}, dimensions={0} | all-to-all | bytes 262144 | tf_op jit(solution)/shard_map/all_to_all | solution.py:340
  216.8 6.3 %collective-permute-start.45 = (f32[256,128]{1,0:T(8,128)S(1)}, f32[256,128]{1,0:T(8,128)S(1)}, u32[]{:S(2)}, u32[]{:S(2)}) collective-permute-start(f32[256,128]{1,0:T(8,128)S(1)} %bitcast.32), channel_id=1, source_target_pairs={{0,1},{1,0},{2,3},{3,2},{4,5},{5,4},{6,7},{7,6},{8,9},{9,8},{10,11... | collective-permute-start | bytes 393224 | tf_op jit(solution)/shard_map/ppermute | solution.py:324
  230.3 10.6 %shard_map.88.before.inv = f32[256,256]{1,0:T(8,128)S(1)} custom-call(s32[4]{0:T(128)S(1)} %pad_add_fusion.1.refs_6_.before.pos, f32[256,128]{1,0:T(8,128)S(1)} %bitcast.33, f32[256,128]{1,0:T(8,128)S(1)} %get-tuple-element.110.other), custom_call_target="tpu_custom_call" | custom-call | flops 1000000 | bytes 100000 | tf_op jit(solution)/shard_map/pallas_call | solution.py:307
  242.2 3.7 collective-permute-done.48.d
  254.8 10.1 %all_to_all.58 = f32[8,32,128]{2,1,0:T(8,128)S(1)} all-to-all(f32[8,32,128]{2,1,0:T(8,128)S(1)} %bitcast.40), channel_id=1, replica_groups=mesh['y'=4,'z'=8,'col'=4,'rep'=2] {'z'}, dimensions={0} | all-to-all | bytes 262144 | tf_op jit(solution)/shard_map/all_to_all | solution.py:340
  281.5 5.2 %collective-permute-done.58.far_part = f32[32,128]{1,0:T(8,128)S(1)} collective-permute-done((f32[32,128]{1,0:T(8,128)S(1)}, f32[32,128]{1,0:T(8,128)S(1)}, u32[]{:S(2)}, u32[]{:S(2)}) %collective-permute-start.58) | collective-permute-done | bytes 16416 | tf_op jit(solution)/shard_map/ppermute | solution.py:324
  290.4 10.3 %all_to_all.59 = f32[8,32,128]{2,1,0:T(8,128)S(1)} all-to-all(f32[8,32,128]{2,1,0:T(8,128)S(1)} %get-tuple-element.120), channel_id=1, replica_groups=mesh['y'=4,'z'=8,'col'=4,'rep'=2] {'z'}, dimensions={0} | all-to-all | bytes 262144 | tf_op jit(solution)/shard_map/all_to_all | solution.py:340
  302.6 4.5 collective-permute-start.62
  307.1 4.8 %collective-permute-start.63 = (f32[256,128]{1,0:T(8,128)S(1)}, f32[256,128]{1,0:T(8,128)S(1)}, u32[]{:S(2)}, u32[]{:S(2)}) collective-permute-start(f32[256,128]{1,0:T(8,128)S(1)} %get-tuple-element.126.own), channel_id=1, source_target_pairs={{0,1},{1,0},{2,3},{3,2},{4,5},{5,4},{6,7},{7,6},{8,9},{9,8},{10,11... | collective-permute-start | bytes 393224 | tf_op jit(solution)/shard_map/ppermute | solution.py:324
  312.9 10.6 %shard_map.95.before.inv = f32[256,256]{1,0:T(8,128)S(1)} custom-call(s32[4]{0:T(128)S(1)} %pad_add_fusion.1.refs_6_.before.pos, f32[256,128]{1,0:T(8,128)S(1)} %get-tuple-element.126.own, f32[256,128]{1,0:T(8,128)S(1)} %collective-permute-done.63.other), custom_call_target="tpu_custom_call" | custom-call | flops 1000000 | bytes 100000 | tf_op jit(solution)/shard_map/pallas_call | solution.py:307
  332.6 4.2 all-to-all-start.6
  339.4 3.0 collective-permute-done.69.down.refs_4_
  344.8 3.6 collective-permute-start.71
  348.4 3.3 collective-permute-start.67
  355.2 3.2 collective-permute-done.73.c
  366.9 14.1 %all_to_all.60 = f32[8,32,128]{2,1,0:T(8,128)S(1)} all-to-all(f32[8,32,128]{2,1,0:T(8,128)S(1)} %shard_map.102), channel_id=1, replica_groups=mesh['y'=4,'z'=8,'col'=4,'rep'=2] {'z'}, dimensions={0} | all-to-all | bytes 262144 | tf_op jit(solution)/shard_map/all_to_all | solution.py:340
  381.1 3.0 collective-permute-start.81
  384.1 6.1 %collective-permute-start.82 = (f32[256,128]{1,0:T(8,128)S(1)}, f32[256,128]{1,0:T(8,128)S(1)}, u32[]{:S(2)}, u32[]{:S(2)}) collective-permute-start(f32[256,128]{1,0:T(8,128)S(1)} %bitcast.29), channel_id=1, source_target_pairs={{0,1},{1,0},{2,3},{3,2},{4,5},{5,4},{6,7},{7,6},{8,9},{9,8},{10,11... | collective-permute-start | bytes 393224 | tf_op jit(solution)/shard_map/ppermute | solution.py:324
  397.4 10.6 %shard_map.105.inv = f32[256,256]{1,0:T(8,128)S(1)} custom-call(s32[4]{0:T(128)S(1)} %pad_add_fusion.1.refs_6_.before.pos, f32[256,128]{1,0:T(8,128)S(1)} %bitcast.30, f32[256,128]{1,0:T(8,128)S(1)} %get-tuple-element.142.other), custom_call_target="tpu_custom_call" | custom-call | flops 1000000 | bytes 100000 | tf_op jit(solution)/shard_map/pallas_call | solution.py:307
  409.5 3.3 collective-permute-done.85.d
  419.7 11.7 %all_to_all.61 = f32[16,16,128]{2,1,0:T(8,128)S(1)} all-to-all(f32[16,16,128]{2,1,0:T(8,128)S(1)} %bitcast.41), channel_id=1, replica_groups=mesh['y'=4,'z'=8,'col'=4,'rep'=2] {'y','col'}, dimensions={0} | all-to-all | bytes 262144 | tf_op jit(solution)/shard_map/all_to_all | solution.py:420
  431.5 9.7 %all_to_all.62 = f32[8,16,128]{2,1,0:T(8,128)S(1)} all-to-all(f32[8,16,128]{2,1,0:T(8,128)S(1)} %broadcast_in_dim.8), channel_id=1, replica_groups=mesh['y'=4,'z'=8,'col'=4,'rep'=2] {'z'}, dimensions={0} | all-to-all | bytes 131072 | tf_op jit(solution)/shard_map/all_to_all | solution.py:422
  441.2 9.8 %all_to_all.63 = f32[16,16,128]{2,1,0:T(8,128)S(1)} all-to-all(f32[16,16,128]{2,1,0:T(8,128)S(1)} %broadcast_in_dim.9), channel_id=1, replica_groups=mesh['y'=4,'z'=8,'col'=4,'rep'=2] {'y','col'}, dimensions={0} | all-to-all | bytes 262144 | tf_op jit(solution)/shard_map/all_to_all | solution.py:424
  451.0 4.1 collective-permute-start.87
  456.1 10.6 %shard_map.109.inv = f32[256,256]{1,0:T(8,128)S(1)} custom-call(s32[4]{0:T(128)S(1)} %pad_add_fusion.1.refs_6_.before.pos, f32[256,128]{1,0:T(8,128)S(1)} %bitcast.37, f32[256,128]{1,0:T(8,128)S(1)} %collective-permute-done.87.other), custom_call_target="tpu_custom_call" | custom-call | flops 1000000 | bytes 100000 | tf_op jit(solution)/shard_map/pallas_call | solution.py:307
  (203 shorter events, 151.9 us)
Async XLA Ops:
  0.7 8.3 %collective-permute-start.2 = (f32[160,128]{1,0:T(8,128)}, f32[160,128]{1,0:T(8,128)S(1)}, u32[]{:S(2)}, u32[]{:S(2)}) collective-permute-start(f32[160,128]{1,0:T(8,128)} %bitcast.8.own.refs_3_), channel_id=1, source_target_pairs={{0,56},{8,0},{16,8},{24,16},{32,24},{40,32},{48,40},{56,48},{1,57}... | collective-permute-start | bytes 245768 | tf_op jit(solution)/shard_map/ppermute | solution.py:324
  12.8 11.8 %collective-permute-start.3 = (f32[320,128]{1,0:T(8,128)S(1)}, f32[320,128]{1,0:T(8,128)S(1)}, u32[]{:S(2)}, u32[]{:S(2)}) collective-permute-start(f32[320,128]{1,0:T(8,128)S(1)} %get-tuple-element.74), channel_id=1, source_target_pairs={{0,16},{8,24},{16,32},{24,40},{32,48},{40,56},{48,0},{56,8},{1,17}... | collective-permute-start | bytes 491528 | tf_op jit(solution)/shard_map/ppermute | solution.py:324
  12.9 11.7 %collective-permute-start.4 = (f32[320,128]{1,0:T(8,128)S(1)}, f32[320,128]{1,0:T(8,128)S(1)}, u32[]{:S(2)}, u32[]{:S(2)}) collective-permute-start(f32[320,128]{1,0:T(8,128)S(1)} %get-tuple-element.75), channel_id=1, source_target_pairs={{0,48},{8,56},{16,0},{24,8},{32,16},{40,24},{48,32},{56,40},{1,49}... | collective-permute-start | bytes 491528 | tf_op jit(solution)/shard_map/ppermute | solution.py:324
  25.5 12.8 %collective-permute-start.6 = (f32[1280,128]{1,0:T(8,128)S(1)}, f32[1280,128]{1,0:T(8,128)S(1)}, u32[]{:S(2)}, u32[]{:S(2)}) collective-permute-start(f32[1280,128]{1,0:T(8,128)S(1)} %shard_map.69.line), channel_id=1, source_target_pairs={{0,192},{64,0},{128,64},{192,128},{1,193},{65,1},{129,65},{193,129... | collective-permute-start | bytes 1966088 | tf_op jit(solution)/shard_map/ppermute | solution.py:324
  28.3 13.1 %collective-permute-start.5 = (f32[1280,128]{1,0:T(8,128)S(1)}, f32[1280,128]{1,0:T(8,128)S(1)}, u32[]{:S(2)}, u32[]{:S(2)}) collective-permute-start(f32[1280,128]{1,0:T(8,128)S(1)} %shard_map.69.line), channel_id=1, source_target_pairs={{0,64},{64,128},{128,192},{192,0},{1,65},{65,129},{129,193},{193,1... | collective-permute-start | bytes 1966088 | tf_op jit(solution)/shard_map/ppermute | solution.py:324
  53.5 13.4 %collective-permute-start.10 = (f32[768,128]{1,0:T(8,128)S(1)}, f32[768,128]{1,0:T(8,128)S(1)}, u32[]{:S(2)}, u32[]{:S(2)}) collective-permute-start(f32[768,128]{1,0:T(8,128)S(1)} %get-tuple-element.80), channel_id=1, source_target_pairs={{0,4},{2,6},{4,0},{6,2},{1,5},{3,7},{5,1},{7,3},{8,12},{10,14},{12... | collective-permute-start | bytes 1179656 | tf_op jit(solution)/shard_map/ppermute | solution.py:324
  55.9 11.0 %collective-permute-start.11 = (f32[768,128]{1,0:T(8,128)S(1)}, f32[768,128]{1,0:T(8,128)S(1)}, u32[]{:S(2)}, u32[]{:S(2)}) collective-permute-start(f32[768,128]{1,0:T(8,128)S(1)} %get-tuple-element.81), channel_id=1, source_target_pairs={{0,6},{2,0},{4,2},{6,4},{1,7},{3,1},{5,3},{7,5},{8,14},{10,8},{12,... | collective-permute-start | bytes 1179656 | tf_op jit(solution)/shard_map/ppermute | solution.py:324
  67.0 11.2 %collective-permute-start.15 = (f32[768,128]{1,0:T(8,128)S(1)}, f32[768,128]{1,0:T(8,128)S(1)}, u32[]{:S(2)}, u32[]{:S(2)}) collective-permute-start(f32[768,128]{1,0:T(8,128)S(1)} %shard_map.72.own.p0), channel_id=1, source_target_pairs={{0,1},{1,0},{2,3},{3,2},{4,5},{5,4},{6,7},{7,6},{8,9},{9,8},{10,11... | collective-permute-start | bytes 1179656 | tf_op jit(solution)/shard_map/ppermute | solution.py:324
  74.6 28.3 %collective-permute-start.14 = (f32[768,128]{1,0:T(8,128)S(1)}, f32[768,128]{1,0:T(8,128)S(1)}, u32[]{:S(2)}, u32[]{:S(2)}) collective-permute-start(f32[768,128]{1,0:T(8,128)S(1)} %shard_map.72.own.p0), channel_id=1, source_target_pairs={{0,6},{2,0},{4,2},{6,4},{1,7},{3,1},{5,3},{7,5},{8,14},{10,8},{12,... | collective-permute-start | bytes 1179656 | tf_op jit(solution)/shard_map/ppermute | solution.py:324
  76.6 26.3 %collective-permute-start.13 = (f32[768,128]{1,0:T(8,128)S(1)}, f32[768,128]{1,0:T(8,128)S(1)}, u32[]{:S(2)}, u32[]{:S(2)}) collective-permute-start(f32[768,128]{1,0:T(8,128)S(1)} %shard_map.72.own.p0), channel_id=1, source_target_pairs={{0,4},{2,6},{4,0},{6,2},{1,5},{3,7},{5,1},{7,3},{8,12},{10,14},{12... | collective-permute-start | bytes 1179656 | tf_op jit(solution)/shard_map/ppermute | solution.py:324
  77.5 25.5 %collective-permute-start.12 = (f32[768,128]{1,0:T(8,128)S(1)}, f32[768,128]{1,0:T(8,128)}, u32[]{:S(2)}, u32[]{:S(2)}) collective-permute-start(f32[768,128]{1,0:T(8,128)S(1)} %shard_map.72.own.p0), channel_id=1, source_target_pairs={{0,2},{2,4},{4,6},{6,0},{1,3},{3,5},{5,7},{7,1},{8,10},{10,12},{12... | collective-permute-start | bytes 1179656 | tf_op jit(solution)/shard_map/ppermute | solution.py:324
  105.8 8.5 %collective-permute-start.19 = (f32[672,128]{1,0:T(8,128)S(1)}, f32[672,128]{1,0:T(8,128)S(1)}, u32[]{:S(2)}, u32[]{:S(2)}) collective-permute-start(f32[672,128]{1,0:T(8,128)S(1)} %get-tuple-element.84), channel_id=1, source_target_pairs={{0,64},{64,128},{128,192},{192,0},{1,65},{65,129},{129,193},{193,1... | collective-permute-start | bytes 1032200 | tf_op jit(solution)/shard_map/ppermute | solution.py:324
  105.9 8.4 %collective-permute-start.20 = (f32[672,128]{1,0:T(8,128)S(1)}, f32[672,128]{1,0:T(8,128)S(1)}, u32[]{:S(2)}, u32[]{:S(2)}) collective-permute-start(f32[672,128]{1,0:T(8,128)S(1)} %get-tuple-element.86), channel_id=1, source_target_pairs={{0,192},{64,0},{128,64},{192,128},{1,193},{65,1},{129,65},{193,129... | collective-permute-start | bytes 1032200 | tf_op jit(solution)/shard_map/ppermute | solution.py:324
  114.4 16.1 %collective-permute-start.22 = (f32[1280,128]{1,0:T(8,128)S(1)}, f32[1280,128]{1,0:T(8,128)S(1)}, u32[]{:S(2)}, u32[]{:S(2)}) collective-permute-start(f32[1280,128]{1,0:T(8,128)S(1)} %get-tuple-element.87), channel_id=1, source_target_pairs={{0,64},{64,128},{128,192},{192,0},{1,65},{65,129},{129,193},{193,1... | collective-permute-start | bytes 1966088 | tf_op jit(solution)/shard_map/ppermute | solution.py:324
  115.4 15.0 %collective-permute-start.23 = (f32[1280,128]{1,0:T(8,128)S(1)}, f32[1280,128]{1,0:T(8,128)S(1)}, u32[]{:S(2)}, u32[]{:S(2)}) collective-permute-start(f32[1280,128]{1,0:T(8,128)S(1)} %get-tuple-element.88), channel_id=1, source_target_pairs={{0,192},{64,0},{128,64},{192,128},{1,193},{65,1},{129,65},{193,129... | collective-permute-start | bytes 1966088 | tf_op jit(solution)/shard_map/ppermute | solution.py:324
  131.1 21.8 %collective-permute-start.24 = (f32[480,128]{1,0:T(8,128)S(1)}, f32[480,128]{1,0:T(8,128)S(1)}, u32[]{:S(2)}, u32[]{:S(2)}) collective-permute-start(f32[480,128]{1,0:T(8,128)S(1)} %get-tuple-element.93), channel_id=1, source_target_pairs={{0,24},{8,32},{16,40},{24,48},{32,56},{40,0},{48,8},{56,16},{1,25}... | collective-permute-start | bytes 737288 | tf_op jit(solution)/shard_map/ppermute | solution.py:324
  131.3 21.6 %collective-permute-start.25 = (f32[320,128]{1,0:T(8,128)S(1)}, f32[320,128]{1,0:T(8,128)S(1)}, u32[]{:S(2)}, u32[]{:S(2)}) collective-permute-start(f32[320,128]{1,0:T(8,128)S(1)} %get-tuple-element.94), channel_id=1, source_target_pairs={{0,40},{8,48},{16,56},{24,0},{32,8},{40,16},{48,24},{56,32},{1,41}... | collective-permute-start | bytes 491528 | tf_op jit(solution)/shard_map/ppermute | solution.py:324
  162.1 12.3 %all-to-all-start.2 = ((f32[8,32,128]{2,1,0:T(8,128)}), f32[8,32,128]{2,1,0:T(8,128)S(1)}, u32[]{:S(2)}, u32[]{:S(2)}) async-start(f32[8,32,128]{2,1,0:T(8,128)} %bitcast.12), calls=%async_computation.2 | async-start | bytes 262144 | tf_op jit(solution)/shard_map/all_to_all | solution.py:340
  174.4 14.0 %collective-permute-start.33 = (f32[320,128]{1,0:T(8,128)S(1)}, f32[320,128]{1,0:T(8,128)S(1)}, u32[]{:S(2)}, u32[]{:S(2)}) collective-permute-start(f32[320,128]{1,0:T(8,128)S(1)} %get-tuple-element.101), channel_id=1, source_target_pairs={{0,16},{8,24},{16,32},{24,40},{32,48},{40,56},{48,0},{56,8},{1,17}... | collective-permute-start | bytes 491528 | tf_op jit(solution)/shard_map/ppermute | solution.py:324
  174.5 14.0 %collective-permute-start.34 = (f32[320,128]{1,0:T(8,128)S(1)}, f32[320,128]{1,0:T(8,128)S(1)}, u32[]{:S(2)}, u32[]{:S(2)}) collective-permute-start(f32[320,128]{1,0:T(8,128)S(1)} %get-tuple-element.102), channel_id=1, source_target_pairs={{0,48},{8,56},{16,0},{24,8},{32,16},{40,24},{48,32},{56,40},{1,49}... | collective-permute-start | bytes 491528 | tf_op jit(solution)/shard_map/ppermute | solution.py:324
  178.0 10.4 %collective-permute-start.30 = (f32[160,128]{1,0:T(8,128)S(1)}, f32[160,128]{1,0:T(8,128)S(1)}, u32[]{:S(2)}, u32[]{:S(2)}) collective-permute-start(f32[160,128]{1,0:T(8,128)S(1)} %get-tuple-element.99.own.refs_3_), channel_id=1, source_target_pairs={{0,32},{8,40},{16,48},{24,56},{32,0},{40,8},{48,16},{56,24},{1,33}... | collective-permute-start | bytes 245768 | tf_op jit(solution)/shard_map/ppermute | solution.py:324
  188.5 25.1 %collective-permute-start.39 = (f32[1280,128]{1,0:T(8,128)S(1)}, f32[1280,128]{1,0:T(8,128)S(1)}, u32[]{:S(2)}, u32[]{:S(2)}) collective-permute-start(f32[1280,128]{1,0:T(8,128)S(1)} %shard_map.84.line), channel_id=1, source_target_pairs={{0,192},{64,0},{128,64},{192,128},{1,193},{65,1},{129,65},{193,129... | collective-permute-start | bytes 1966088 | tf_op jit(solution)/shard_map/ppermute | solution.py:324
  190.0 23.5 %collective-permute-start.38 = (f32[1280,128]{1,0:T(8,128)S(1)}, f32[1280,128]{1,0:T(8,128)S(1)}, u32[]{:S(2)}, u32[]{:S(2)}) collective-permute-start(f32[1280,128]{1,0:T(8,128)S(1)} %shard_map.84.line), channel_id=1, source_target_pairs={{0,64},{64,128},{128,192},{192,0},{1,65},{65,129},{129,193},{193,1... | collective-permute-start | bytes 1966088 | tf_op jit(solution)/shard_map/ppermute | solution.py:324
  213.6 10.4 %collective-permute-start.43 = (f32[640,128]{1,0:T(8,128)S(1)}, f32[640,128]{1,0:T(8,128)S(1)}, u32[]{:S(2)}, u32[]{:S(2)}) collective-permute-start(f32[640,128]{1,0:T(8,128)S(1)} %get-tuple-element.104), channel_id=1, source_target_pairs={{0,64},{64,128},{128,192},{192,0},{1,65},{65,129},{129,193},{193,1... | collective-permute-start | bytes 983048 | tf_op jit(solution)/shard_map/ppermute | solution.py:324
  215.2 8.9 %collective-permute-start.44 = (f32[640,128]{1,0:T(8,128)S(1)}, f32[640,128]{1,0:T(8,128)S(1)}, u32[]{:S(2)}, u32[]{:S(2)}) collective-permute-start(f32[640,128]{1,0:T(8,128)S(1)} %get-tuple-element.105), channel_id=1, source_target_pairs={{0,192},{64,0},{128,64},{192,128},{1,193},{65,1},{129,65},{193,129... | collective-permute-start | bytes 983048 | tf_op jit(solution)/shard_map/ppermute | solution.py:324
  226.4 14.5 %collective-permute-start.46 = (f32[768,128]{1,0:T(8,128)S(1)}, f32[768,128]{1,0:T(8,128)S(1)}, u32[]{:S(2)}, u32[]{:S(2)}) collective-permute-start(f32[768,128]{1,0:T(8,128)S(1)} %get-tuple-element.107), channel_id=1, source_target_pairs={{0,2},{2,4},{4,6},{6,0},{1,3},{3,5},{5,7},{7,1},{8,10},{10,12},{12... | collective-permute-start | bytes 1179656 | tf_op jit(solution)/shard_map/ppermute | solution.py:324
  226.5 15.7 %collective-permute-start.47 = (f32[768,128]{1,0:T(8,128)S(1)}, f32[768,128]{1,0:T(8,128)S(1)}, u32[]{:S(2)}, u32[]{:S(2)}) collective-permute-start(f32[768,128]{1,0:T(8,128)S(1)} %get-tuple-element.108), channel_id=1, source_target_pairs={{0,4},{2,6},{4,0},{6,2},{1,5},{3,7},{5,1},{7,3},{8,12},{10,14},{12... | collective-permute-start | bytes 1179656 | tf_op jit(solution)/shard_map/ppermute | solution.py:324
  228.3 17.6 %collective-permute-start.48 = (f32[768,128]{1,0:T(8,128)S(1)}, f32[768,128]{1,0:T(8,128)S(1)}, u32[]{:S(2)}, u32[]{:S(2)}) collective-permute-start(f32[768,128]{1,0:T(8,128)S(1)} %get-tuple-element.109), channel_id=1, source_target_pairs={{0,6},{2,0},{4,2},{6,4},{1,7},{3,1},{5,3},{7,5},{8,14},{10,8},{12,... | collective-permute-start | bytes 1179656 | tf_op jit(solution)/shard_map/ppermute | solution.py:324
  251.7 24.0 %collective-permute-start.52 = (f32[768,128]{1,0:T(8,128)S(1)}, f32[768,128]{1,0:T(8,128)S(1)}, u32[]{:S(2)}, u32[]{:S(2)}) collective-permute-start(f32[768,128]{1,0:T(8,128)S(1)} %get-tuple-element.111.p0), channel_id=1, source_target_pairs={{0,6},{2,0},{4,2},{6,4},{1,7},{3,1},{5,3},{7,5},{8,14},{10,8},{12,... | collective-permute-start | bytes 1179656 | tf_op jit(solution)/shard_map/ppermute | solution.py:324
  254.1 21.6 %collective-permute-start.51 = (f32[768,128]{1,0:T(8,128)S(1)}, f32[768,128]{1,0:T(8,128)S(1)}, u32[]{:S(2)}, u32[]{:S(2)}) collective-permute-start(f32[768,128]{1,0:T(8,128)S(1)} %get-tuple-element.111.p0), channel_id=1, source_target_pairs={{0,4},{2,6},{4,0},{6,2},{1,5},{3,7},{5,1},{7,3},{8,12},{10,14},{12... | collective-permute-start | bytes 1179656 | tf_op jit(solution)/shard_map/ppermute | solution.py:324
  254.6 21.1 %collective-permute-start.50 = (f32[768,128]{1,0:T(8,128)S(1)}, f32[768,128]{1,0:T(8,128)}, u32[]{:S(2)}, u32[]{:S(2)}) collective-permute-start(f32[768,128]{1,0:T(8,128)S(1)} %get-tuple-element.111.p0), channel_id=1, source_target_pairs={{0,2},{2,4},{4,6},{6,0},{1,3},{3,5},{5,7},{7,1},{8,10},{10,12},{12... | collective-permute-start | bytes 1179656 | tf_op jit(solution)/shard_map/ppermute | solution.py:324
  278.6 8.9 %collective-permute-start.56 = (f32[672,128]{1,0:T(8,128)S(1)}, f32[672,128]{1,0:T(8,128)S(1)}, u32[]{:S(2)}, u32[]{:S(2)}) collective-permute-start(f32[672,128]{1,0:T(8,128)S(1)} %get-tuple-element.115), channel_id=1, source_target_pairs={{0,64},{64,128},{128,192},{192,0},{1,65},{65,129},{129,193},{193,1... | collective-permute-start | bytes 1032200 | tf_op jit(solution)/shard_map/ppermute | solution.py:324
  278.9 8.7 %collective-permute-start.57 = (f32[672,128]{1,0:T(8,128)S(1)}, f32[672,128]{1,0:T(8,128)S(1)}, u32[]{:S(2)}, u32[]{:S(2)}) collective-permute-start(f32[672,128]{1,0:T(8,128)S(1)} %get-tuple-element.117), channel_id=1, source_target_pairs={{0,192},{64,0},{128,64},{192,128},{1,193},{65,1},{129,65},{193,129... | collective-permute-start | bytes 1032200 | tf_op jit(solution)/shard_map/ppermute | solution.py:324
  287.7 14.2 %collective-permute-start.59 = (f32[1280,128]{1,0:T(8,128)S(1)}, f32[1280,128]{1,0:T(8,128)S(1)}, u32[]{:S(2)}, u32[]{:S(2)}) collective-permute-start(f32[1280,128]{1,0:T(8,128)S(1)} %get-tuple-element.118), channel_id=1, source_target_pairs={{0,64},{64,128},{128,192},{192,0},{1,65},{65,129},{129,193},{193,1... | collective-permute-start | bytes 1966088 | tf_op jit(solution)/shard_map/ppermute | solution.py:324
  288.2 13.6 %collective-permute-start.60 = (f32[1280,128]{1,0:T(8,128)S(1)}, f32[1280,128]{1,0:T(8,128)S(1)}, u32[]{:S(2)}, u32[]{:S(2)}) collective-permute-start(f32[1280,128]{1,0:T(8,128)S(1)} %get-tuple-element.119), channel_id=1, source_target_pairs={{0,192},{64,0},{128,64},{192,128},{1,193},{65,1},{129,65},{193,129... | collective-permute-start | bytes 1966088 | tf_op jit(solution)/shard_map/ppermute | solution.py:324
  302.5 21.0 %collective-permute-start.61 = (f32[480,128]{1,0:T(8,128)S(1)}, f32[480,128]{1,0:T(8,128)S(1)}, u32[]{:S(2)}, u32[]{:S(2)}) collective-permute-start(f32[480,128]{1,0:T(8,128)S(1)} %get-tuple-element.124), channel_id=1, source_target_pairs={{0,24},{8,32},{16,40},{24,48},{32,56},{40,0},{48,8},{56,16},{1,25}... | collective-permute-start | bytes 737288 | tf_op jit(solution)/shard_map/ppermute | solution.py:324
  302.6 20.9 %collective-permute-start.62 = (f32[320,128]{1,0:T(8,128)S(1)}, f32[320,128]{1,0:T(8,128)S(1)}, u32[]{:S(2)}, u32[]{:S(2)}) collective-permute-start(f32[320,128]{1,0:T(8,128)S(1)} %get-tuple-element.125), channel_id=1, source_target_pairs={{0,40},{8,48},{16,56},{24,0},{32,8},{40,16},{48,24},{56,32},{1,41}... | collective-permute-start | bytes 491528 | tf_op jit(solution)/shard_map/ppermute | solution.py:324
  332.6 12.1 %all-to-all-start.6 = ((f32[8,32,128]{2,1,0:T(8,128)}), f32[8,32,128]{2,1,0:T(8,128)S(1)}, u32[]{:S(2)}, u32[]{:S(2)}) async-start(f32[8,32,128]{2,1,0:T(8,128)} %bitcast.16), calls=%async_computation.6 | async-start | bytes 262144 | tf_op jit(solution)/shard_map/all_to_all | solution.py:340
  344.7 15.1 %collective-permute-start.70 = (f32[320,128]{1,0:T(8,128)S(1)}, f32[320,128]{1,0:T(8,128)S(1)}, u32[]{:S(2)}, u32[]{:S(2)}) collective-permute-start(f32[320,128]{1,0:T(8,128)S(1)} %get-tuple-element.132), channel_id=1, source_target_pairs={{0,16},{8,24},{16,32},{24,40},{32,48},{40,56},{48,0},{56,8},{1,17}... | collective-permute-start | bytes 491528 | tf_op jit(solution)/shard_map/ppermute | solution.py:324
  344.8 15.1 %collective-permute-start.71 = (f32[320,128]{1,0:T(8,128)S(1)}, f32[320,128]{1,0:T(8,128)S(1)}, u32[]{:S(2)}, u32[]{:S(2)}) collective-permute-start(f32[320,128]{1,0:T(8,128)S(1)} %get-tuple-element.133), channel_id=1, source_target_pairs={{0,48},{8,56},{16,0},{24,8},{32,16},{40,24},{48,32},{56,40},{1,49}... | collective-permute-start | bytes 491528 | tf_op jit(solution)/shard_map/ppermute | solution.py:324
  348.4 11.5 %collective-permute-start.67 = (f32[160,128]{1,0:T(8,128)S(1)}, f32[160,128]{1,0:T(8,128)S(1)}, u32[]{:S(2)}, u32[]{:S(2)}) collective-permute-start(f32[160,128]{1,0:T(8,128)S(1)} %get-tuple-element.130.own.refs_3_), channel_id=1, source_target_pairs={{0,32},{8,40},{16,48},{24,56},{32,0},{40,8},{48,16},{56,24},{1,33}... | collective-permute-start | bytes 245768 | tf_op jit(solution)/shard_map/ppermute | solution.py:324
  359.9 21.0 %collective-permute-start.76 = (f32[1280,128]{1,0:T(8,128)S(1)}, f32[1280,128]{1,0:T(8,128)S(1)}, u32[]{:S(2)}, u32[]{:S(2)}) collective-permute-start(f32[1280,128]{1,0:T(8,128)S(1)} %shard_map.101.line), channel_id=1, source_target_pairs={{0,192},{64,0},{128,64},{192,128},{1,193},{65,1},{129,65},{193,129... | collective-permute-start | bytes 1966088 | tf_op jit(solution)/shard_map/ppermute | solution.py:324
  361.5 19.5 %collective-permute-start.75 = (f32[1280,128]{1,0:T(8,128)S(1)}, f32[1280,128]{1,0:T(8,128)S(1)}, u32[]{:S(2)}, u32[]{:S(2)}) collective-permute-start(f32[1280,128]{1,0:T(8,128)S(1)} %shard_map.101.line), channel_id=1, source_target_pairs={{0,64},{64,128},{128,192},{192,0},{1,65},{65,129},{129,193},{193,1... | collective-permute-start | bytes 1966088 | tf_op jit(solution)/shard_map/ppermute | solution.py:324
  381.0 10.2 %collective-permute-start.80 = (f32[640,128]{1,0:T(8,128)S(1)}, f32[640,128]{1,0:T(8,128)S(1)}, u32[]{:S(2)}, u32[]{:S(2)}) collective-permute-start(f32[640,128]{1,0:T(8,128)S(1)} %get-tuple-element.135), channel_id=1, source_target_pairs={{0,64},{64,128},{128,192},{192,0},{1,65},{65,129},{129,193},{193,1... | collective-permute-start | bytes 983048 | tf_op jit(solution)/shard_map/ppermute | solution.py:324
  381.1 10.1 %collective-permute-start.81 = (f32[640,128]{1,0:T(8,128)S(1)}, f32[640,128]{1,0:T(8,128)S(1)}, u32[]{:S(2)}, u32[]{:S(2)}) collective-permute-start(f32[640,128]{1,0:T(8,128)S(1)} %get-tuple-element.136), channel_id=1, source_target_pairs={{0,192},{64,0},{128,64},{192,128},{1,193},{65,1},{129,65},{193,129... | collective-permute-start | bytes 983048 | tf_op jit(solution)/shard_map/ppermute | solution.py:324
  393.6 16.0 %collective-permute-start.83 = (f32[768,128]{1,0:T(8,128)S(1)}, f32[768,128]{1,0:T(8,128)S(1)}, u32[]{:S(2)}, u32[]{:S(2)}) collective-permute-start(f32[768,128]{1,0:T(8,128)S(1)} %get-tuple-element.138), channel_id=1, source_target_pairs={{0,2},{2,4},{4,6},{6,0},{1,3},{3,5},{5,7},{7,1},{8,10},{10,12},{12... | collective-permute-start | bytes 1179656 | tf_op jit(solution)/shard_map/ppermute | solution.py:324
  393.7 15.8 %collective-permute-start.84 = (f32[768,128]{1,0:T(8,128)S(1)}, f32[768,128]{1,0:T(8,128)S(1)}, u32[]{:S(2)}, u32[]{:S(2)}) collective-permute-start(f32[768,128]{1,0:T(8,128)S(1)} %get-tuple-element.139), channel_id=1, source_target_pairs={{0,4},{2,6},{4,0},{6,2},{1,5},{3,7},{5,1},{7,3},{8,12},{10,14},{12... | collective-permute-start | bytes 1179656 | tf_op jit(solution)/shard_map/ppermute | solution.py:324
  396.0 16.8 %collective-permute-start.85 = (f32[768,128]{1,0:T(8,128)S(1)}, f32[768,128]{1,0:T(8,128)S(1)}, u32[]{:S(2)}, u32[]{:S(2)}) collective-permute-start(f32[768,128]{1,0:T(8,128)S(1)} %get-tuple-element.140), channel_id=1, source_target_pairs={{0,6},{2,0},{4,2},{6,4},{1,7},{3,1},{5,3},{7,5},{8,14},{10,8},{12,... | collective-permute-start | bytes 1179656 | tf_op jit(solution)/shard_map/ppermute | solution.py:324
  (47 other events, 390.8 us)
where the time goes:
time: 478 us; the launch traced here: 469 us
  starting transfers between devices  165 us (35%)
  waiting for transfers between devices  110 us (23%)
  blocking collectives  109 us (23%)
  Pallas kernels  82.3 us (17%)
    ppermute x88, starting transfers between devices, send(): return lax.ppermute(value, axis, ring(size, shift))  156 us
    ppermute x88, waiting for transfers between devices, send(): return lax.ppermute(value, axis, ring(size, shift))  109 us
    pallas_call x43, Pallas kernels, call(): pl.pallas_call(kernel, out_shape=[jax.ShapeDtypeStruct(shape, F32) for sh...  82.3 us
    all_to_all x6, blocking collectives, exchange_z(): return lax.all_to_all(parts, 'z', 0, 0)  77.8 us
    all_to_all x1, blocking collectives, sum_gram(): parts = lax.all_to_all(gram.reshape(count, chunk, HALF), ('y', 'col'), 0, 0)  11.7 us
    all_to_all x1, blocking collectives, sum_gram(): lax.all_to_all(jnp.broadcast_to(part[None], (count, chunk, HALF)), ('y',...  9.82 us
    all_to_all x1, blocking collectives, sum_gram(): lax.all_to_all(jnp.broadcast_to(part[None], (NZ, chunk, HALF)), 'z', 0, 0)  9.71 us
  transfers between devices with their start and end apart: 90, of which 47 were waited for; matrix products, arithmetic and copies ran while one was open for 0% of the time, Pallas kernels for 10%

commit v1 on v0

--- a/solution.py
+++ b/solution.py
@@ -127,8 +127,11 @@
     high[COLS_OWN:, :] = down[...]
 
 
-def fan_kernel(up, own, down, parts, low, high, total):
+def fan_kernel(up, own, down, before, low, high):
     pair_kernel(up, own, down, low, high)
+
+
+def sum_parts_kernel(parts, total):
     value = parts[0]
     for k in range(1, parts.shape[0]):
         value = value + parts[k]
@@ -353,8 +356,9 @@
     def gather_panel(own, gram):
         up, down, far = (send(own, "z", k) for k in (1, NZ - 1, 4))
         parts = exchange_z(gram.reshape(chunks))
-        low, high, part = call(
-            fan_kernel, [(2 * COLS_OWN, HALF)] * 2 + [chunks[1:]], [], [up, own, down, parts]
+        part = call(sum_parts_kernel, [chunks[1:]], [], [parts])[0]
+        low, high = call(
+            fan_kernel, [(2 * COLS_OWN, HALF)] * 2, [], [up, own, down], (), [part]
         )
         line = [far, send(low, "z", 2), up, own, down, send(high, "z", NZ - 2)]
         part = sum_ring(part, "y")

time: 478 us -> 478 us (level)
    ppermute x88, waiting for transfers between devices: 109 us -> 99.1 us  [send(): return lax.ppermute(value, axis, ring(size, shift))]
    all_to_all x2, waiting for transfers between devices: 0.4 us -> 10.5 us  [exchange_z(): return lax.all_to_all(parts, 'z', 0, 0)]
    pallas_call x43 -> x45, Pallas kernels: 82.3 us -> 82.3 us  [call(): pl.pallas_call(kernel, out_shape=[jax.ShapeDtypeStruct(shape, F32) for sh...]
  transfers between devices with their start and end apart: 90 -> 90, of which waited for: 47 -> 43; matrix products, arithmetic and copies ran while one was open for 0% -> 0% of each run, Pallas kernels for 10% -> 10%
where the time goes in v1:
time: 478 us; the launch traced here: 469 us
  starting transfers between devices  165 us (35%)
  waiting for transfers between devices  110 us (23%)
  blocking collectives  109 us (23%)
  Pallas kernels  82.3 us (17%)
    ppermute x88, starting transfers between devices, send(): return lax.ppermute(value, axis, ring(size, shift))  156 us
    ppermute x88, waiting for transfers between devices, send(): return lax.ppermute(value, axis, ring(size, shift))  99.1 us
    pallas_call x45, Pallas kernels, call(): pl.pallas_call(kernel, out_shape=[jax.ShapeDtypeStruct(shape, F32) for sh...  82.3 us
    all_to_all x6, blocking collectives, exchange_z(): return lax.all_to_all(parts, 'z', 0, 0)  77.8 us
    all_to_all x1, blocking collectives, sum_gram(): parts = lax.all_to_all(gram.reshape(count, chunk, HALF), ('y', 'col'), 0, 0)  11.7 us
    all_to_all x2, waiting for transfers between devices, exchange_z(): return lax.all_to_all(parts, 'z', 0, 0)  10.5 us
    all_to_all x1, blocking collectives, sum_gram(): lax.all_to_all(jnp.broadcast_to(part[None], (count, chunk, HALF)), ('y',...  9.82 us
    all_to_all x1, blocking collectives, sum_gram(): lax.all_to_all(jnp.broadcast_to(part[None], (NZ, chunk, HALF)), 'z', 0, 0)  9.71 us
  transfers between devices with their start and end apart: 90, of which 43 were waited for; matrix products, arithmetic and copies ran while one was open for 0% of the time, Pallas kernels for 10%

profile of v1, /device:TPU:1, one launch (start us, length us, event | category | flops | bytes accessed | tf_op | source)
XLA Modules:
  0.0 469.0 jit_solution(2969953235396447901)
XLA Ops:
  0.7 6.5 %collective-permute-start.2 = (f32[160,128]{1,0:T(8,128)}, f32[160,128]{1,0:T(8,128)S(1)}, u32[]{:S(2)}, u32[]{:S(2)}) collective-permute-start(f32[160,128]{1,0:T(8,128)} %bitcast.8.own.refs_3_), channel_id=1, source_target_pairs={{0,56},{8,0},{16,8},{24,16},{32,24},{40,32},{48,40},{56,48},{1,57}... | collective-permute-start | bytes 245768 | tf_op jit(solution)/shard_map/ppermute | solution.py:327
  9.0 2.9 collective-permute-done.1.up.refs_2_
  12.9 3.6 collective-permute-start.4
  17.9 6.6 %collective-permute-done.refs_0_ = f32[160,128]{1,0:T(8,128)S(1)} collective-permute-done((f32[160,128]{1,0:T(8,128)}, f32[160,128]{1,0:T(8,128)S(1)}, u32[]{:S(2)}, u32[]{:S(2)}) %collective-permute-start) | collective-permute-done | bytes 81952 | tf_op jit(solution)/shard_map/ppermute | solution.py:327
  28.3 10.0 %collective-permute-done.6.back.after = f32[1280,128]{1,0:T(8,128)S(1)} collective-permute-done((f32[1280,128]{1,0:T(8,128)S(1)}, f32[1280,128]{1,0:T(8,128)S(1)}, u32[]{:S(2)}, u32[]{:S(2)}) %collective-permute-start.6) | collective-permute-done | bytes 655392 | tf_op jit(solution)/shard_map/ppermute | solution.py:327
  38.3 3.1 collective-permute-done.5.after_that.before
  45.0 4.5 collective-permute-done.7.far_a
  57.1 3.0 collective-permute-done.9.b
  60.1 6.8 %collective-permute-done.10.c = f32[768,128]{1,0:T(8,128)S(1)} collective-permute-done((f32[768,128]{1,0:T(8,128)S(1)}, f32[768,128]{1,0:T(8,128)S(1)}, u32[]{:S(2)}, u32[]{:S(2)}) %collective-permute-start.10) | collective-permute-done | bytes 393248 | tf_op jit(solution)/shard_map/ppermute | solution.py:327
  67.0 7.6 %collective-permute-start.15 = (f32[768,128]{1,0:T(8,128)S(1)}, f32[768,128]{1,0:T(8,128)S(1)}, u32[]{:S(2)}, u32[]{:S(2)}) collective-permute-start(f32[768,128]{1,0:T(8,128)S(1)} %shard_map.72.own.p0), channel_id=1, source_target_pairs={{0,1},{1,0},{2,3},{3,2},{4,5},{5,4},{6,7},{7,6},{8,9},{9,8},{10,11... | collective-permute-start | bytes 1179656 | tf_op jit(solution)/shard_map/ppermute | solution.py:327
  79.6 16.0 %all_to_all.55 = f32[8,32,128]{2,1,0:T(8,128)S(1)} all-to-all(f32[8,32,128]{2,1,0:T(8,128)S(1)} %bitcast.38), channel_id=1, replica_groups=mesh['y'=4,'z'=8,'col'=4,'rep'=2] {'z'}, dimensions={0} | all-to-all | bytes 262144 | tf_op jit(solution)/shard_map/all_to_all | solution.py:343
  109.5 4.8 %collective-permute-done.21.far_part = f32[32,128]{1,0:T(8,128)S(1)} collective-permute-done((f32[32,128]{1,0:T(8,128)S(1)}, f32[32,128]{1,0:T(8,128)S(1)}, u32[]{:S(2)}, u32[]{:S(2)}) %collective-permute-start.21) | collective-permute-done | bytes 16416 | tf_op jit(solution)/shard_map/ppermute | solution.py:327
  117.2 13.3 %all_to_all.56 = f32[8,32,128]{2,1,0:T(8,128)S(1)} all-to-all(f32[8,32,128]{2,1,0:T(8,128)S(1)} %get-tuple-element.87), channel_id=1, replica_groups=mesh['y'=4,'z'=8,'col'=4,'rep'=2] {'z'}, dimensions={0} | all-to-all | bytes 262144 | tf_op jit(solution)/shard_map/all_to_all | solution.py:343
  131.3 4.4 collective-permute-start.25
  135.7 5.7 %collective-permute-start.26 = (f32[256,128]{1,0:T(8,128)S(1)}, f32[256,128]{1,0:T(8,128)S(1)}, u32[]{:S(2)}, u32[]{:S(2)}) collective-permute-start(f32[256,128]{1,0:T(8,128)S(1)} %get-tuple-element.93.own), channel_id=1, source_target_pairs={{0,1},{1,0},{2,3},{3,2},{4,5},{5,4},{6,7},{7,6},{8,9},{9,8},{10,11... | collective-permute-start | bytes 393224 | tf_op jit(solution)/shard_map/ppermute | solution.py:327
  142.4 10.6 %shard_map.78.before.inv = f32[256,256]{1,0:T(8,128)S(1)} custom-call(s32[4]{0:T(128)S(1)} %pad_add_fusion.1.refs_6_.before.pos, f32[256,128]{1,0:T(8,128)S(1)} %get-tuple-element.93.own, f32[256,128]{1,0:T(8,128)S(1)} %collective-permute-done.26.other), custom_call_target="tpu_custom_call" | custom-call | flops 1000000 | bytes 100000 | tf_op jit(solution)/shard_map/pallas_call | solution.py:310
  162.1 4.3 all-to-all-start.2
  169.1 5.3 %all-to-all-done.2.parts = f32[8,32,128]{2,1,0:T(8,128)S(1)} async-done(((f32[8,32,128]{2,1,0:T(8,128)}), f32[8,32,128]{2,1,0:T(8,128)S(1)}, u32[]{:S(2)}, u32[]{:S(2)}) %all-to-all-start.2) | async-done | bytes 131104 | tf_op jit(solution)/shard_map/all_to_all | solution.py:343
  174.5 3.6 collective-permute-start.34
  178.1 3.0 collective-permute-start.30
  184.1 3.2 collective-permute-done.36.c
  190.0 5.4 %collective-permute-start.42 = (f32[32,128]{1,0:T(8,128)S(1)}, f32[32,128]{1,0:T(8,128)S(1)}, u32[]{:S(2)}, u32[]{:S(2)}) collective-permute-start(f32[32,128]{1,0:T(8,128)S(1)} %shard_map.84.refs_6_.a), channel_id=1, source_target_pairs={{0,6},{2,0},{4,2},{6,4},{1,7},{3,1},{5,3},{7,5},{8,14},{10,8},{12,... | collective-permute-start | bytes 49160 | tf_op jit(solution)/shard_map/ppermute | solution.py:327
  196.3 3.2 collective-permute-done.41.c
  199.5 14.0 %all_to_all.57 = f32[8,32,128]{2,1,0:T(8,128)S(1)} all-to-all(f32[8,32,128]{2,1,0:T(8,128)S(1)} %shard_map.86), channel_id=1, replica_groups=mesh['y'=4,'z'=8,'col'=4,'rep'=2] {'z'}, dimensions={0} | all-to-all | bytes 262144 | tf_op jit(solution)/shard_map/all_to_all | solution.py:343
  216.7 6.3 %collective-permute-start.45 = (f32[256,128]{1,0:T(8,128)S(1)}, f32[256,128]{1,0:T(8,128)S(1)}, u32[]{:S(2)}, u32[]{:S(2)}) collective-permute-start(f32[256,128]{1,0:T(8,128)S(1)} %bitcast.32), channel_id=1, source_target_pairs={{0,1},{1,0},{2,3},{3,2},{4,5},{5,4},{6,7},{7,6},{8,9},{9,8},{10,11... | collective-permute-start | bytes 393224 | tf_op jit(solution)/shard_map/ppermute | solution.py:327
  230.3 10.6 %shard_map.89.before.inv = f32[256,256]{1,0:T(8,128)S(1)} custom-call(s32[4]{0:T(128)S(1)} %pad_add_fusion.1.refs_6_.before.pos, f32[256,128]{1,0:T(8,128)S(1)} %bitcast.33, f32[256,128]{1,0:T(8,128)S(1)} %get-tuple-element.107.other), custom_call_target="tpu_custom_call" | custom-call | flops 1000000 | bytes 100000 | tf_op jit(solution)/shard_map/pallas_call | solution.py:310
  242.2 3.7 collective-permute-done.48.d
  254.8 10.1 %all_to_all.58 = f32[8,32,128]{2,1,0:T(8,128)S(1)} all-to-all(f32[8,32,128]{2,1,0:T(8,128)S(1)} %bitcast.40), channel_id=1, replica_groups=mesh['y'=4,'z'=8,'col'=4,'rep'=2] {'z'}, dimensions={0} | all-to-all | bytes 262144 | tf_op jit(solution)/shard_map/all_to_all | solution.py:343
  281.5 5.2 %collective-permute-done.58.far_part = f32[32,128]{1,0:T(8,128)S(1)} collective-permute-done((f32[32,128]{1,0:T(8,128)S(1)}, f32[32,128]{1,0:T(8,128)S(1)}, u32[]{:S(2)}, u32[]{:S(2)}) %collective-permute-start.58) | collective-permute-done | bytes 16416 | tf_op jit(solution)/shard_map/ppermute | solution.py:327
  290.4 10.3 %all_to_all.59 = f32[8,32,128]{2,1,0:T(8,128)S(1)} all-to-all(f32[8,32,128]{2,1,0:T(8,128)S(1)} %get-tuple-element.117), channel_id=1, replica_groups=mesh['y'=4,'z'=8,'col'=4,'rep'=2] {'z'}, dimensions={0} | all-to-all | bytes 262144 | tf_op jit(solution)/shard_map/all_to_all | solution.py:343
  302.6 4.5 collective-permute-start.62
  307.0 4.8 %collective-permute-start.63 = (f32[256,128]{1,0:T(8,128)S(1)}, f32[256,128]{1,0:T(8,128)S(1)}, u32[]{:S(2)}, u32[]{:S(2)}) collective-permute-start(f32[256,128]{1,0:T(8,128)S(1)} %get-tuple-element.123.own), channel_id=1, source_target_pairs={{0,1},{1,0},{2,3},{3,2},{4,5},{5,4},{6,7},{7,6},{8,9},{9,8},{10,11... | collective-permute-start | bytes 393224 | tf_op jit(solution)/shard_map/ppermute | solution.py:327
  312.9 10.6 %shard_map.96.before.inv = f32[256,256]{1,0:T(8,128)S(1)} custom-call(s32[4]{0:T(128)S(1)} %pad_add_fusion.1.refs_6_.before.pos, f32[256,128]{1,0:T(8,128)S(1)} %get-tuple-element.123.own, f32[256,128]{1,0:T(8,128)S(1)} %collective-permute-done.63.other), custom_call_target="tpu_custom_call" | custom-call | flops 1000000 | bytes 100000 | tf_op jit(solution)/shard_map/pallas_call | solution.py:310
  332.6 4.2 all-to-all-start.6
  339.4 5.3 %all-to-all-done.6.parts = f32[8,32,128]{2,1,0:T(8,128)S(1)} async-done(((f32[8,32,128]{2,1,0:T(8,128)}), f32[8,32,128]{2,1,0:T(8,128)S(1)}, u32[]{:S(2)}, u32[]{:S(2)}) %all-to-all-start.6) | async-done | bytes 131104 | tf_op jit(solution)/shard_map/all_to_all | solution.py:343
  344.8 3.6 collective-permute-start.71
  348.4 3.2 collective-permute-start.67
  355.2 3.2 collective-permute-done.73.c
  366.9 14.1 %all_to_all.60 = f32[8,32,128]{2,1,0:T(8,128)S(1)} all-to-all(f32[8,32,128]{2,1,0:T(8,128)S(1)} %shard_map.104), channel_id=1, replica_groups=mesh['y'=4,'z'=8,'col'=4,'rep'=2] {'z'}, dimensions={0} | all-to-all | bytes 262144 | tf_op jit(solution)/shard_map/all_to_all | solution.py:343
  381.1 3.0 collective-permute-start.81
  384.1 6.1 %collective-permute-start.82 = (f32[256,128]{1,0:T(8,128)S(1)}, f32[256,128]{1,0:T(8,128)S(1)}, u32[]{:S(2)}, u32[]{:S(2)}) collective-permute-start(f32[256,128]{1,0:T(8,128)S(1)} %bitcast.29), channel_id=1, source_target_pairs={{0,1},{1,0},{2,3},{3,2},{4,5},{5,4},{6,7},{7,6},{8,9},{9,8},{10,11... | collective-permute-start | bytes 393224 | tf_op jit(solution)/shard_map/ppermute | solution.py:327
  397.5 10.6 %shard_map.107.inv = f32[256,256]{1,0:T(8,128)S(1)} custom-call(s32[4]{0:T(128)S(1)} %pad_add_fusion.1.refs_6_.before.pos, f32[256,128]{1,0:T(8,128)S(1)} %bitcast.30, f32[256,128]{1,0:T(8,128)S(1)} %get-tuple-element.138.other), custom_call_target="tpu_custom_call" | custom-call | flops 1000000 | bytes 100000 | tf_op jit(solution)/shard_map/pallas_call | solution.py:310
  409.6 3.3 collective-permute-done.85.d
  419.8 11.7 %all_to_all.61 = f32[16,16,128]{2,1,0:T(8,128)S(1)} all-to-all(f32[16,16,128]{2,1,0:T(8,128)S(1)} %bitcast.41), channel_id=1, replica_groups=mesh['y'=4,'z'=8,'col'=4,'rep'=2] {'y','col'}, dimensions={0} | all-to-all | bytes 262144 | tf_op jit(solution)/shard_map/all_to_all | solution.py:424
  431.5 9.7 %all_to_all.62 = f32[8,16,128]{2,1,0:T(8,128)S(1)} all-to-all(f32[8,16,128]{2,1,0:T(8,128)S(1)} %broadcast_in_dim.8), channel_id=1, replica_groups=mesh['y'=4,'z'=8,'col'=4,'rep'=2] {'z'}, dimensions={0} | all-to-all | bytes 131072 | tf_op jit(solution)/shard_map/all_to_all | solution.py:426
  441.3 9.8 %all_to_all.63 = f32[16,16,128]{2,1,0:T(8,128)S(1)} all-to-all(f32[16,16,128]{2,1,0:T(8,128)S(1)} %broadcast_in_dim.9), channel_id=1, replica_groups=mesh['y'=4,'z'=8,'col'=4,'rep'=2] {'y','col'}, dimensions={0} | all-to-all | bytes 262144 | tf_op jit(solution)/shard_map/all_to_all | solution.py:428
  451.1 4.1 collective-permute-start.87
  456.2 10.6 %shard_map.111.inv = f32[256,256]{1,0:T(8,128)S(1)} custom-call(s32[4]{0:T(128)S(1)} %pad_add_fusion.1.refs_6_.before.pos, f32[256,128]{1,0:T(8,128)S(1)} %bitcast.37, f32[256,128]{1,0:T(8,128)S(1)} %collective-permute-done.87.other), custom_call_target="tpu_custom_call" | custom-call | flops 1000000 | bytes 100000 | tf_op jit(solution)/shard_map/pallas_call | solution.py:310
  (205 shorter events, 147.3 us)
Async XLA Ops:
  0.7 8.3 %collective-permute-start.2 = (f32[160,128]{1,0:T(8,128)}, f32[160,128]{1,0:T(8,128)S(1)}, u32[]{:S(2)}, u32[]{:S(2)}) collective-permute-start(f32[160,128]{1,0:T(8,128)} %bitcast.8.own.refs_3_), channel_id=1, source_target_pairs={{0,56},{8,0},{16,8},{24,16},{32,24},{40,32},{48,40},{56,48},{1,57}... | collective-permute-start | bytes 245768 | tf_op jit(solution)/shard_map/ppermute | solution.py:327
  12.8 11.8 %collective-permute-start.3 = (f32[320,128]{1,0:T(8,128)S(1)}, f32[320,128]{1,0:T(8,128)S(1)}, u32[]{:S(2)}, u32[]{:S(2)}) collective-permute-start(f32[320,128]{1,0:T(8,128)S(1)} %get-tuple-element.72), channel_id=1, source_target_pairs={{0,16},{8,24},{16,32},{24,40},{32,48},{40,56},{48,0},{56,8},{1,17}... | collective-permute-start | bytes 491528 | tf_op jit(solution)/shard_map/ppermute | solution.py:327
  12.9 11.7 %collective-permute-start.4 = (f32[320,128]{1,0:T(8,128)S(1)}, f32[320,128]{1,0:T(8,128)S(1)}, u32[]{:S(2)}, u32[]{:S(2)}) collective-permute-start(f32[320,128]{1,0:T(8,128)S(1)} %get-tuple-element.73), channel_id=1, source_target_pairs={{0,48},{8,56},{16,0},{24,8},{32,16},{40,24},{48,32},{56,40},{1,49}... | collective-permute-start | bytes 491528 | tf_op jit(solution)/shard_map/ppermute | solution.py:327
  25.5 12.8 %collective-permute-start.6 = (f32[1280,128]{1,0:T(8,128)S(1)}, f32[1280,128]{1,0:T(8,128)S(1)}, u32[]{:S(2)}, u32[]{:S(2)}) collective-permute-start(f32[1280,128]{1,0:T(8,128)S(1)} %shard_map.69.line), channel_id=1, source_target_pairs={{0,192},{64,0},{128,64},{192,128},{1,193},{65,1},{129,65},{193,129... | collective-permute-start | bytes 1966088 | tf_op jit(solution)/shard_map/ppermute | solution.py:327
  28.3 13.1 %collective-permute-start.5 = (f32[1280,128]{1,0:T(8,128)S(1)}, f32[1280,128]{1,0:T(8,128)S(1)}, u32[]{:S(2)}, u32[]{:S(2)}) collective-permute-start(f32[1280,128]{1,0:T(8,128)S(1)} %shard_map.69.line), channel_id=1, source_target_pairs={{0,64},{64,128},{128,192},{192,0},{1,65},{65,129},{129,193},{193,1... | collective-permute-start | bytes 1966088 | tf_op jit(solution)/shard_map/ppermute | solution.py:327
  53.5 13.4 %collective-permute-start.10 = (f32[768,128]{1,0:T(8,128)S(1)}, f32[768,128]{1,0:T(8,128)S(1)}, u32[]{:S(2)}, u32[]{:S(2)}) collective-permute-start(f32[768,128]{1,0:T(8,128)S(1)} %get-tuple-element.78), channel_id=1, source_target_pairs={{0,4},{2,6},{4,0},{6,2},{1,5},{3,7},{5,1},{7,3},{8,12},{10,14},{12... | collective-permute-start | bytes 1179656 | tf_op jit(solution)/shard_map/ppermute | solution.py:327
  55.9 11.0 %collective-permute-start.11 = (f32[768,128]{1,0:T(8,128)S(1)}, f32[768,128]{1,0:T(8,128)S(1)}, u32[]{:S(2)}, u32[]{:S(2)}) collective-permute-start(f32[768,128]{1,0:T(8,128)S(1)} %get-tuple-element.79), channel_id=1, source_target_pairs={{0,6},{2,0},{4,2},{6,4},{1,7},{3,1},{5,3},{7,5},{8,14},{10,8},{12,... | collective-permute-start | bytes 1179656 | tf_op jit(solution)/shard_map/ppermute | solution.py:327
  67.0 11.2 %collective-permute-start.15 = (f32[768,128]{1,0:T(8,128)S(1)}, f32[768,128]{1,0:T(8,128)S(1)}, u32[]{:S(2)}, u32[]{:S(2)}) collective-permute-start(f32[768,128]{1,0:T(8,128)S(1)} %shard_map.72.own.p0), channel_id=1, source_target_pairs={{0,1},{1,0},{2,3},{3,2},{4,5},{5,4},{6,7},{7,6},{8,9},{9,8},{10,11... | collective-permute-start | bytes 1179656 | tf_op jit(solution)/shard_map/ppermute | solution.py:327
  74.6 28.3 %collective-permute-start.14 = (f32[768,128]{1,0:T(8,128)S(1)}, f32[768,128]{1,0:T(8,128)S(1)}, u32[]{:S(2)}, u32[]{:S(2)}) collective-permute-start(f32[768,128]{1,0:T(8,128)S(1)} %shard_map.72.own.p0), channel_id=1, source_target_pairs={{0,6},{2,0},{4,2},{6,4},{1,7},{3,1},{5,3},{7,5},{8,14},{10,8},{12,... | collective-permute-start | bytes 1179656 | tf_op jit(solution)/shard_map/ppermute | solution.py:327
  76.6 26.3 %collective-permute-start.13 = (f32[768,128]{1,0:T(8,128)S(1)}, f32[768,128]{1,0:T(8,128)S(1)}, u32[]{:S(2)}, u32[]{:S(2)}) collective-permute-start(f32[768,128]{1,0:T(8,128)S(1)} %shard_map.72.own.p0), channel_id=1, source_target_pairs={{0,4},{2,6},{4,0},{6,2},{1,5},{3,7},{5,1},{7,3},{8,12},{10,14},{12... | collective-permute-start | bytes 1179656 | tf_op jit(solution)/shard_map/ppermute | solution.py:327
  77.5 25.5 %collective-permute-start.12 = (f32[768,128]{1,0:T(8,128)S(1)}, f32[768,128]{1,0:T(8,128)}, u32[]{:S(2)}, u32[]{:S(2)}) collective-permute-start(f32[768,128]{1,0:T(8,128)S(1)} %shard_map.72.own.p0), channel_id=1, source_target_pairs={{0,2},{2,4},{4,6},{6,0},{1,3},{3,5},{5,7},{7,1},{8,10},{10,12},{12... | collective-permute-start | bytes 1179656 | tf_op jit(solution)/shard_map/ppermute | solution.py:327
  105.8 8.5 %collective-permute-start.19 = (f32[672,128]{1,0:T(8,128)S(1)}, f32[672,128]{1,0:T(8,128)S(1)}, u32[]{:S(2)}, u32[]{:S(2)}) collective-permute-start(f32[672,128]{1,0:T(8,128)S(1)} %get-tuple-element.82), channel_id=1, source_target_pairs={{0,64},{64,128},{128,192},{192,0},{1,65},{65,129},{129,193},{193,1... | collective-permute-start | bytes 1032200 | tf_op jit(solution)/shard_map/ppermute | solution.py:327
  105.9 8.4 %collective-permute-start.20 = (f32[672,128]{1,0:T(8,128)S(1)}, f32[672,128]{1,0:T(8,128)S(1)}, u32[]{:S(2)}, u32[]{:S(2)}) collective-permute-start(f32[672,128]{1,0:T(8,128)S(1)} %get-tuple-element.84), channel_id=1, source_target_pairs={{0,192},{64,0},{128,64},{192,128},{1,193},{65,1},{129,65},{193,129... | collective-permute-start | bytes 1032200 | tf_op jit(solution)/shard_map/ppermute | solution.py:327
  114.4 16.1 %collective-permute-start.22 = (f32[1280,128]{1,0:T(8,128)S(1)}, f32[1280,128]{1,0:T(8,128)S(1)}, u32[]{:S(2)}, u32[]{:S(2)}) collective-permute-start(f32[1280,128]{1,0:T(8,128)S(1)} %get-tuple-element.85), channel_id=1, source_target_pairs={{0,64},{64,128},{128,192},{192,0},{1,65},{65,129},{129,193},{193,1... | collective-permute-start | bytes 1966088 | tf_op jit(solution)/shard_map/ppermute | solution.py:327
  115.4 15.0 %collective-permute-start.23 = (f32[1280,128]{1,0:T(8,128)S(1)}, f32[1280,128]{1,0:T(8,128)S(1)}, u32[]{:S(2)}, u32[]{:S(2)}) collective-permute-start(f32[1280,128]{1,0:T(8,128)S(1)} %get-tuple-element.86), channel_id=1, source_target_pairs={{0,192},{64,0},{128,64},{192,128},{1,193},{65,1},{129,65},{193,129... | collective-permute-start | bytes 1966088 | tf_op jit(solution)/shard_map/ppermute | solution.py:327
  131.1 21.8 %collective-permute-start.24 = (f32[480,128]{1,0:T(8,128)S(1)}, f32[480,128]{1,0:T(8,128)S(1)}, u32[]{:S(2)}, u32[]{:S(2)}) collective-permute-start(f32[480,128]{1,0:T(8,128)S(1)} %get-tuple-element.91), channel_id=1, source_target_pairs={{0,24},{8,32},{16,40},{24,48},{32,56},{40,0},{48,8},{56,16},{1,25}... | collective-permute-start | bytes 737288 | tf_op jit(solution)/shard_map/ppermute | solution.py:327
  131.3 21.6 %collective-permute-start.25 = (f32[320,128]{1,0:T(8,128)S(1)}, f32[320,128]{1,0:T(8,128)S(1)}, u32[]{:S(2)}, u32[]{:S(2)}) collective-permute-start(f32[320,128]{1,0:T(8,128)S(1)} %get-tuple-element.92), channel_id=1, source_target_pairs={{0,40},{8,48},{16,56},{24,0},{32,8},{40,16},{48,24},{56,32},{1,41}... | collective-permute-start | bytes 491528 | tf_op jit(solution)/shard_map/ppermute | solution.py:327
  162.1 12.3 %all-to-all-start.2 = ((f32[8,32,128]{2,1,0:T(8,128)}), f32[8,32,128]{2,1,0:T(8,128)S(1)}, u32[]{:S(2)}, u32[]{:S(2)}) async-start(f32[8,32,128]{2,1,0:T(8,128)} %bitcast.12), calls=%async_computation.2 | async-start | bytes 262144 | tf_op jit(solution)/shard_map/all_to_all | solution.py:343
  174.4 14.0 %collective-permute-start.33 = (f32[320,128]{1,0:T(8,128)S(1)}, f32[320,128]{1,0:T(8,128)S(1)}, u32[]{:S(2)}, u32[]{:S(2)}) collective-permute-start(f32[320,128]{1,0:T(8,128)S(1)} %get-tuple-element.99), channel_id=1, source_target_pairs={{0,16},{8,24},{16,32},{24,40},{32,48},{40,56},{48,0},{56,8},{1,17}... | collective-permute-start | bytes 491528 | tf_op jit(solution)/shard_map/ppermute | solution.py:327
  174.5 13.9 %collective-permute-start.34 = (f32[320,128]{1,0:T(8,128)S(1)}, f32[320,128]{1,0:T(8,128)S(1)}, u32[]{:S(2)}, u32[]{:S(2)}) collective-permute-start(f32[320,128]{1,0:T(8,128)S(1)} %get-tuple-element.100), channel_id=1, source_target_pairs={{0,48},{8,56},{16,0},{24,8},{32,16},{40,24},{48,32},{56,40},{1,49}... | collective-permute-start | bytes 491528 | tf_op jit(solution)/shard_map/ppermute | solution.py:327
  178.1 10.3 %collective-permute-start.30 = (f32[160,128]{1,0:T(8,128)S(1)}, f32[160,128]{1,0:T(8,128)S(1)}, u32[]{:S(2)}, u32[]{:S(2)}) collective-permute-start(f32[160,128]{1,0:T(8,128)S(1)} %get-tuple-element.97.own.refs_3_), channel_id=1, source_target_pairs={{0,32},{8,40},{16,48},{24,56},{32,0},{40,8},{48,16},{56,24},{1,33}... | collective-permute-start | bytes 245768 | tf_op jit(solution)/shard_map/ppermute | solution.py:327
  188.5 25.1 %collective-permute-start.39 = (f32[1280,128]{1,0:T(8,128)S(1)}, f32[1280,128]{1,0:T(8,128)S(1)}, u32[]{:S(2)}, u32[]{:S(2)}) collective-permute-start(f32[1280,128]{1,0:T(8,128)S(1)} %shard_map.85.line), channel_id=1, source_target_pairs={{0,192},{64,0},{128,64},{192,128},{1,193},{65,1},{129,65},{193,129... | collective-permute-start | bytes 1966088 | tf_op jit(solution)/shard_map/ppermute | solution.py:327
  190.0 23.5 %collective-permute-start.38 = (f32[1280,128]{1,0:T(8,128)S(1)}, f32[1280,128]{1,0:T(8,128)S(1)}, u32[]{:S(2)}, u32[]{:S(2)}) collective-permute-start(f32[1280,128]{1,0:T(8,128)S(1)} %shard_map.85.line), channel_id=1, source_target_pairs={{0,64},{64,128},{128,192},{192,0},{1,65},{65,129},{129,193},{193,1... | collective-permute-start | bytes 1966088 | tf_op jit(solution)/shard_map/ppermute | solution.py:327
  213.6 10.5 %collective-permute-start.43 = (f32[640,128]{1,0:T(8,128)S(1)}, f32[640,128]{1,0:T(8,128)S(1)}, u32[]{:S(2)}, u32[]{:S(2)}) collective-permute-start(f32[640,128]{1,0:T(8,128)S(1)} %get-tuple-element.101), channel_id=1, source_target_pairs={{0,64},{64,128},{128,192},{192,0},{1,65},{65,129},{129,193},{193,1... | collective-permute-start | bytes 983048 | tf_op jit(solution)/shard_map/ppermute | solution.py:327
  215.1 9.0 %collective-permute-start.44 = (f32[640,128]{1,0:T(8,128)S(1)}, f32[640,128]{1,0:T(8,128)S(1)}, u32[]{:S(2)}, u32[]{:S(2)}) collective-permute-start(f32[640,128]{1,0:T(8,128)S(1)} %get-tuple-element.102), channel_id=1, source_target_pairs={{0,192},{64,0},{128,64},{192,128},{1,193},{65,1},{129,65},{193,129... | collective-permute-start | bytes 983048 | tf_op jit(solution)/shard_map/ppermute | solution.py:327
  226.4 14.5 %collective-permute-start.46 = (f32[768,128]{1,0:T(8,128)S(1)}, f32[768,128]{1,0:T(8,128)S(1)}, u32[]{:S(2)}, u32[]{:S(2)}) collective-permute-start(f32[768,128]{1,0:T(8,128)S(1)} %get-tuple-element.104), channel_id=1, source_target_pairs={{0,2},{2,4},{4,6},{6,0},{1,3},{3,5},{5,7},{7,1},{8,10},{10,12},{12... | collective-permute-start | bytes 1179656 | tf_op jit(solution)/shard_map/ppermute | solution.py:327
  226.5 15.7 %collective-permute-start.47 = (f32[768,128]{1,0:T(8,128)S(1)}, f32[768,128]{1,0:T(8,128)S(1)}, u32[]{:S(2)}, u32[]{:S(2)}) collective-permute-start(f32[768,128]{1,0:T(8,128)S(1)} %get-tuple-element.105), channel_id=1, source_target_pairs={{0,4},{2,6},{4,0},{6,2},{1,5},{3,7},{5,1},{7,3},{8,12},{10,14},{12... | collective-permute-start | bytes 1179656 | tf_op jit(solution)/shard_map/ppermute | solution.py:327
  228.3 17.6 %collective-permute-start.48 = (f32[768,128]{1,0:T(8,128)S(1)}, f32[768,128]{1,0:T(8,128)S(1)}, u32[]{:S(2)}, u32[]{:S(2)}) collective-permute-start(f32[768,128]{1,0:T(8,128)S(1)} %get-tuple-element.106), channel_id=1, source_target_pairs={{0,6},{2,0},{4,2},{6,4},{1,7},{3,1},{5,3},{7,5},{8,14},{10,8},{12,... | collective-permute-start | bytes 1179656 | tf_op jit(solution)/shard_map/ppermute | solution.py:327
  251.7 24.0 %collective-permute-start.52 = (f32[768,128]{1,0:T(8,128)S(1)}, f32[768,128]{1,0:T(8,128)S(1)}, u32[]{:S(2)}, u32[]{:S(2)}) collective-permute-start(f32[768,128]{1,0:T(8,128)S(1)} %get-tuple-element.108.p0), channel_id=1, source_target_pairs={{0,6},{2,0},{4,2},{6,4},{1,7},{3,1},{5,3},{7,5},{8,14},{10,8},{12,... | collective-permute-start | bytes 1179656 | tf_op jit(solution)/shard_map/ppermute | solution.py:327
  254.1 21.6 %collective-permute-start.51 = (f32[768,128]{1,0:T(8,128)S(1)}, f32[768,128]{1,0:T(8,128)S(1)}, u32[]{:S(2)}, u32[]{:S(2)}) collective-permute-start(f32[768,128]{1,0:T(8,128)S(1)} %get-tuple-element.108.p0), channel_id=1, source_target_pairs={{0,4},{2,6},{4,0},{6,2},{1,5},{3,7},{5,1},{7,3},{8,12},{10,14},{12... | collective-permute-start | bytes 1179656 | tf_op jit(solution)/shard_map/ppermute | solution.py:327
  254.6 21.1 %collective-permute-start.50 = (f32[768,128]{1,0:T(8,128)S(1)}, f32[768,128]{1,0:T(8,128)}, u32[]{:S(2)}, u32[]{:S(2)}) collective-permute-start(f32[768,128]{1,0:T(8,128)S(1)} %get-tuple-element.108.p0), channel_id=1, source_target_pairs={{0,2},{2,4},{4,6},{6,0},{1,3},{3,5},{5,7},{7,1},{8,10},{10,12},{12... | collective-permute-start | bytes 1179656 | tf_op jit(solution)/shard_map/ppermute | solution.py:327
  278.6 8.9 %collective-permute-start.56 = (f32[672,128]{1,0:T(8,128)S(1)}, f32[672,128]{1,0:T(8,128)S(1)}, u32[]{:S(2)}, u32[]{:S(2)}) collective-permute-start(f32[672,128]{1,0:T(8,128)S(1)} %get-tuple-element.112), channel_id=1, source_target_pairs={{0,64},{64,128},{128,192},{192,0},{1,65},{65,129},{129,193},{193,1... | collective-permute-start | bytes 1032200 | tf_op jit(solution)/shard_map/ppermute | solution.py:327
  278.9 8.7 %collective-permute-start.57 = (f32[672,128]{1,0:T(8,128)S(1)}, f32[672,128]{1,0:T(8,128)S(1)}, u32[]{:S(2)}, u32[]{:S(2)}) collective-permute-start(f32[672,128]{1,0:T(8,128)S(1)} %get-tuple-element.114), channel_id=1, source_target_pairs={{0,192},{64,0},{128,64},{192,128},{1,193},{65,1},{129,65},{193,129... | collective-permute-start | bytes 1032200 | tf_op jit(solution)/shard_map/ppermute | solution.py:327
  287.7 14.2 %collective-permute-start.59 = (f32[1280,128]{1,0:T(8,128)S(1)}, f32[1280,128]{1,0:T(8,128)S(1)}, u32[]{:S(2)}, u32[]{:S(2)}) collective-permute-start(f32[1280,128]{1,0:T(8,128)S(1)} %get-tuple-element.115), channel_id=1, source_target_pairs={{0,64},{64,128},{128,192},{192,0},{1,65},{65,129},{129,193},{193,1... | collective-permute-start | bytes 1966088 | tf_op jit(solution)/shard_map/ppermute | solution.py:327
  288.2 13.6 %collective-permute-start.60 = (f32[1280,128]{1,0:T(8,128)S(1)}, f32[1280,128]{1,0:T(8,128)S(1)}, u32[]{:S(2)}, u32[]{:S(2)}) collective-permute-start(f32[1280,128]{1,0:T(8,128)S(1)} %get-tuple-element.116), channel_id=1, source_target_pairs={{0,192},{64,0},{128,64},{192,128},{1,193},{65,1},{129,65},{193,129... | collective-permute-start | bytes 1966088 | tf_op jit(solution)/shard_map/ppermute | solution.py:327
  302.5 21.0 %collective-permute-start.61 = (f32[480,128]{1,0:T(8,128)S(1)}, f32[480,128]{1,0:T(8,128)S(1)}, u32[]{:S(2)}, u32[]{:S(2)}) collective-permute-start(f32[480,128]{1,0:T(8,128)S(1)} %get-tuple-element.121), channel_id=1, source_target_pairs={{0,24},{8,32},{16,40},{24,48},{32,56},{40,0},{48,8},{56,16},{1,25}... | collective-permute-start | bytes 737288 | tf_op jit(solution)/shard_map/ppermute | solution.py:327
  302.6 20.9 %collective-permute-start.62 = (f32[320,128]{1,0:T(8,128)S(1)}, f32[320,128]{1,0:T(8,128)S(1)}, u32[]{:S(2)}, u32[]{:S(2)}) collective-permute-start(f32[320,128]{1,0:T(8,128)S(1)} %get-tuple-element.122), channel_id=1, source_target_pairs={{0,40},{8,48},{16,56},{24,0},{32,8},{40,16},{48,24},{56,32},{1,41}... | collective-permute-start | bytes 491528 | tf_op jit(solution)/shard_map/ppermute | solution.py:327
  332.6 12.1 %all-to-all-start.6 = ((f32[8,32,128]{2,1,0:T(8,128)}), f32[8,32,128]{2,1,0:T(8,128)S(1)}, u32[]{:S(2)}, u32[]{:S(2)}) async-start(f32[8,32,128]{2,1,0:T(8,128)} %bitcast.16), calls=%async_computation.6 | async-start | bytes 262144 | tf_op jit(solution)/shard_map/all_to_all | solution.py:343
  344.7 15.1 %collective-permute-start.70 = (f32[320,128]{1,0:T(8,128)S(1)}, f32[320,128]{1,0:T(8,128)S(1)}, u32[]{:S(2)}, u32[]{:S(2)}) collective-permute-start(f32[320,128]{1,0:T(8,128)S(1)} %get-tuple-element.129), channel_id=1, source_target_pairs={{0,16},{8,24},{16,32},{24,40},{32,48},{40,56},{48,0},{56,8},{1,17}... | collective-permute-start | bytes 491528 | tf_op jit(solution)/shard_map/ppermute | solution.py:327
  344.8 15.0 %collective-permute-start.71 = (f32[320,128]{1,0:T(8,128)S(1)}, f32[320,128]{1,0:T(8,128)S(1)}, u32[]{:S(2)}, u32[]{:S(2)}) collective-permute-start(f32[320,128]{1,0:T(8,128)S(1)} %get-tuple-element.130), channel_id=1, source_target_pairs={{0,48},{8,56},{16,0},{24,8},{32,16},{40,24},{48,32},{56,40},{1,49}... | collective-permute-start | bytes 491528 | tf_op jit(solution)/shard_map/ppermute | solution.py:327
  348.4 11.4 %collective-permute-start.67 = (f32[160,128]{1,0:T(8,128)S(1)}, f32[160,128]{1,0:T(8,128)S(1)}, u32[]{:S(2)}, u32[]{:S(2)}) collective-permute-start(f32[160,128]{1,0:T(8,128)S(1)} %get-tuple-element.127.own.refs_3_), channel_id=1, source_target_pairs={{0,32},{8,40},{16,48},{24,56},{32,0},{40,8},{48,16},{56,24},{1,33}... | collective-permute-start | bytes 245768 | tf_op jit(solution)/shard_map/ppermute | solution.py:327
  359.9 21.0 %collective-permute-start.76 = (f32[1280,128]{1,0:T(8,128)S(1)}, f32[1280,128]{1,0:T(8,128)S(1)}, u32[]{:S(2)}, u32[]{:S(2)}) collective-permute-start(f32[1280,128]{1,0:T(8,128)S(1)} %shard_map.103.line), channel_id=1, source_target_pairs={{0,192},{64,0},{128,64},{192,128},{1,193},{65,1},{129,65},{193,129... | collective-permute-start | bytes 1966088 | tf_op jit(solution)/shard_map/ppermute | solution.py:327
  361.5 19.5 %collective-permute-start.75 = (f32[1280,128]{1,0:T(8,128)S(1)}, f32[1280,128]{1,0:T(8,128)S(1)}, u32[]{:S(2)}, u32[]{:S(2)}) collective-permute-start(f32[1280,128]{1,0:T(8,128)S(1)} %shard_map.103.line), channel_id=1, source_target_pairs={{0,64},{64,128},{128,192},{192,0},{1,65},{65,129},{129,193},{193,1... | collective-permute-start | bytes 1966088 | tf_op jit(solution)/shard_map/ppermute | solution.py:327
  381.0 10.3 %collective-permute-start.80 = (f32[640,128]{1,0:T(8,128)S(1)}, f32[640,128]{1,0:T(8,128)S(1)}, u32[]{:S(2)}, u32[]{:S(2)}) collective-permute-start(f32[640,128]{1,0:T(8,128)S(1)} %get-tuple-element.131), channel_id=1, source_target_pairs={{0,64},{64,128},{128,192},{192,0},{1,65},{65,129},{129,193},{193,1... | collective-permute-start | bytes 983048 | tf_op jit(solution)/shard_map/ppermute | solution.py:327
  381.1 10.2 %collective-permute-start.81 = (f32[640,128]{1,0:T(8,128)S(1)}, f32[640,128]{1,0:T(8,128)S(1)}, u32[]{:S(2)}, u32[]{:S(2)}) collective-permute-start(f32[640,128]{1,0:T(8,128)S(1)} %get-tuple-element.132), channel_id=1, source_target_pairs={{0,192},{64,0},{128,64},{192,128},{1,193},{65,1},{129,65},{193,129... | collective-permute-start | bytes 983048 | tf_op jit(solution)/shard_map/ppermute | solution.py:327
  393.6 16.0 %collective-permute-start.83 = (f32[768,128]{1,0:T(8,128)S(1)}, f32[768,128]{1,0:T(8,128)S(1)}, u32[]{:S(2)}, u32[]{:S(2)}) collective-permute-start(f32[768,128]{1,0:T(8,128)S(1)} %get-tuple-element.134), channel_id=1, source_target_pairs={{0,2},{2,4},{4,6},{6,0},{1,3},{3,5},{5,7},{7,1},{8,10},{10,12},{12... | collective-permute-start | bytes 1179656 | tf_op jit(solution)/shard_map/ppermute | solution.py:327
  393.7 15.8 %collective-permute-start.84 = (f32[768,128]{1,0:T(8,128)S(1)}, f32[768,128]{1,0:T(8,128)S(1)}, u32[]{:S(2)}, u32[]{:S(2)}) collective-permute-start(f32[768,128]{1,0:T(8,128)S(1)} %get-tuple-element.135), channel_id=1, source_target_pairs={{0,4},{2,6},{4,0},{6,2},{1,5},{3,7},{5,1},{7,3},{8,12},{10,14},{12... | collective-permute-start | bytes 1179656 | tf_op jit(solution)/shard_map/ppermute | solution.py:327
  396.1 16.8 %collective-permute-start.85 = (f32[768,128]{1,0:T(8,128)S(1)}, f32[768,128]{1,0:T(8,128)S(1)}, u32[]{:S(2)}, u32[]{:S(2)}) collective-permute-start(f32[768,128]{1,0:T(8,128)S(1)} %get-tuple-element.136), channel_id=1, source_target_pairs={{0,6},{2,0},{4,2},{6,4},{1,7},{3,1},{5,3},{7,5},{8,14},{10,8},{12,... | collective-permute-start | bytes 1179656 | tf_op jit(solution)/shard_map/ppermute | solution.py:327
  (47 other events, 395.9 us)
